TPU v7x, 32 devices: a whole 2x2x4 slice. The times are simulated.
32 devices in a mesh: span: 8 (over z, x), ctx: 4 (over y, core).
Axes of the slice: x: 2, y: 2, z: 4, core: 2. Of those that a mesh axis runs over, the one named last changes fastest.
Arguments:
- queries: bfloat16 [4096, 3072], P(('span', 'ctx')), may hold values from -64 to 64
- keys: bfloat16 [4096, 512], P(('span', 'ctx')), may hold values from -16 to 16
- values: bfloat16 [4096, 512], P(('span', 'ctx')), may hold values from -6 to 6
- temps: float32 [8, 24], replicated, may hold values from 0.5 to 2
- levels: int32 [8], replicated, may hold values from 0 to 7
- ctx_list: int32 [8, 4], replicated, may hold values from -1 to 6, as said below
- counts: int32 [8], replicated, may hold values from 256 to 512
Outputs:
- attended: bfloat16 [4096, 3072], P(('span', 'ctx'))
Inputs may be any that keep to these rules, and one draw needn't show every extreme that they name: `ctx_list`: slot 0 of span c's list is c - 1 (-1 for span 0). Slot 1, when used, is span 0. The other slots hold distinct spans below c - 1, used slots first, then -1. The list of span 8 - 1 has no -1.
All inputs are finite; a program needn't handle non-finite values.
Results may differ from a plain program's by a relative error of at most 0.0041.
Values may be sent and summed in bfloat16 or wider, within the bound.
No kernel may reach another device: no remote copies, remote signals or barrier semaphores. Data moves between devices by JAX's collectives and lax.ppermute only.
A program may use at most 128 MiB of HBM per device.

v0:
```python
import math

import jax
import jax.numpy as jnp
from jax import lax
from jax.sharding import PartitionSpec as P

HQ = 24
KVH = 4
HD = 128


def slot_scores(query_group, key_slot, scale_group):
    scores = jnp.einsum("rgd,kd->grk", query_group, key_slot, preferred_element_type=jnp.float32)
    return scores * scale_group[:, None, None]


def row_maxima(query_rows, key_slots, mask, scale):
    group_size = HQ // KVH
    row_count = query_rows.shape[0]
    query_heads = query_rows.reshape(row_count, HQ, HD)
    maxima = []
    for kv_head in range(KVH):
        lower = kv_head * group_size
        query_group = query_heads[:, lower : lower + group_size]
        highest = jnp.full((group_size, row_count), -1e30, jnp.float32)
        for slot_index in range(key_slots.shape[0]):
            scores = slot_scores(
                query_group,
                key_slots[slot_index][:, kv_head * HD : (kv_head + 1) * HD],
                scale[lower : lower + group_size],
            )
            scores = jnp.where(mask[slot_index][None, None, :], scores, -1e30)
            highest = jnp.maximum(highest, jnp.max(scores, axis=-1))
        maxima.append(highest)
    return jnp.concatenate(maxima, axis=0)


def weighted_sums(query_rows, key_slots, value_slots, mask, scale, maxima):
    group_size = HQ // KVH
    row_count = query_rows.shape[0]
    query_heads = query_rows.reshape(row_count, HQ, HD)
    sums_list = []
    totals_list = []
    for kv_head in range(KVH):
        lower = kv_head * group_size
        query_group = query_heads[:, lower : lower + group_size]
        highest = maxima[lower : lower + group_size]
        accum = jnp.zeros((row_count, group_size, HD), jnp.float32)
        totals = jnp.zeros((group_size, row_count), jnp.float32)
        for slot_index in range(key_slots.shape[0]):
            scores = slot_scores(
                query_group,
                key_slots[slot_index][:, kv_head * HD : (kv_head + 1) * HD],
                scale[lower : lower + group_size],
            )
            keep = mask[slot_index][None, None, :]
            scores = jnp.where(keep, scores, -1e30)
            weights = jnp.where(keep, jnp.exp(scores - highest[:, :, None]), 0.0)
            totals = totals + jnp.sum(weights, axis=-1)
            value_group = value_slots[slot_index][:, kv_head * HD : (kv_head + 1) * HD]
            accum = accum + jnp.einsum(
                "grk,kd->rgd",
                weights.astype(jnp.bfloat16),
                value_group,
                preferred_element_type=jnp.float32,
            )
        sums_list.append(accum)
        totals_list.append(totals)
    sums = jnp.concatenate(sums_list, axis=1).reshape(row_count, HQ * HD)
    totals = jnp.transpose(jnp.concatenate(totals_list, axis=0))
    return (sums, totals)


def finish(sums, totals):
    row_count = sums.shape[0]
    result = sums.reshape(row_count, HQ, HD) / totals[:, :, None]
    return result.reshape(row_count, HQ * HD).astype(jnp.bfloat16)


def per_device(queries, keys, values, temps, levels, ctx_list, counts):
    span_index = lax.axis_index("span")
    tok_rows = keys.shape[0]
    width = keys.shape[1]
    wanted = lax.dynamic_index_in_dim(ctx_list, span_index, 0, keepdims=False)
    empty = jnp.zeros((wanted.shape[0], tok_rows, width), keys.dtype)
    piece_keys = lax.all_gather(keys, "span", axis=0, tiled=True)
    piece_values = lax.all_gather(values, "span", axis=0, tiled=True)
    length = piece_keys.shape[0]
    new_keys = []
    new_values = []
    for slot_index in range(wanted.shape[0]):
        source = wanted[slot_index]
        offset = source * tok_rows
        inside = (source >= 0) & (offset >= 0) & (offset + tok_rows <= length)
        begin = jnp.clip(offset, 0, length - tok_rows)
        slab_keys = lax.dynamic_slice_in_dim(piece_keys, begin, tok_rows, 0)
        slab_values = lax.dynamic_slice_in_dim(piece_values, begin, tok_rows, 0)
        new_keys.append(lax.select(inside, slab_keys, empty[slot_index]))
        new_values.append(lax.select(inside, slab_values, empty[slot_index]))
    context_keys = jnp.stack(new_keys)
    context_values = jnp.stack(new_values)
    slot_keys = jnp.concatenate([keys[None], context_keys], axis=0)
    slot_values = jnp.concatenate([values[None], context_values], axis=0)
    span_ids = jnp.concatenate([jnp.reshape(span_index, (1,)), wanted])
    valid_span = span_ids >= 0
    lengths = counts[jnp.maximum(span_ids, 0)]
    level = lax.dynamic_index_in_dim(levels, span_index, 0, keepdims=False)
    scale = lax.dynamic_index_in_dim(temps, level, 0, keepdims=False) / math.sqrt(HD)
    all_keys, all_values = (
        lax.all_gather(slot_keys, "ctx", axis=1, tiled=True),
        lax.all_gather(slot_values, "ctx", axis=1, tiled=True),
    )
    positions = jnp.arange(all_keys.shape[1], dtype=jnp.int32)
    mask = valid_span[:, None] & (positions[None, :] < lengths[:, None])
    maxima = row_maxima(queries, all_keys, mask, scale)
    sums, totals = weighted_sums(queries, all_keys, all_values, mask, scale, maxima)
    return finish(sums, totals)


def solution(mesh):
    return jax.shard_map(
        per_device,
        mesh=mesh,
        in_specs=(
            P(("span", "ctx"), None),
            P(("span", "ctx"), None),
            P(("span", "ctx"), None),
            P(),
            P(),
            P(),
            P(),
        ),
        out_specs=P(("span", "ctx"), None),
        check_vma=False,
    )
```

profile of v0, /device:TPU:25, one launch (start us, length us, event | category | flops | bytes accessed | tf_op | source)
XLA Modules:
  0.0 188.2 jit_solution(4914630517834356614)
XLA Ops:
  6.5 0.7 all-gather.9.cloned.1.call-update
  7.3 0.7 all-gather.5.cloned.1.call-update
  8.1 0.9 fusion.212
  8.9 0.5 fusion.213
  14.4 0.9 bitcast_dynamic-update-slice_fusion.4
  15.3 0.9 bitcast_dynamic-update-slice_fusion.9
  16.2 31.3 %all-gather.9.cloned.1.call-done = bf16[1024,512]{1,0:T(8,128)(2,1)} async-done(((bf16[128,512]{1,0:T(8,128)(2,1)}), bf16[1024,512]{1,0:T(8,128)(2,1)}) %all-gather.9.cloned.1.call-update) | async-done | bytes 1048592 | tf_op jit(solution)/shard_map/all_gather | solution.py:87
  47.5 41.1 %all-gather.5.cloned.1.call-done = bf16[1024,512]{1,0:T(8,128)(2,1)} async-done(((bf16[128,512]{1,0:T(8,128)(2,1)}), bf16[1024,512]{1,0:T(8,128)(2,1)}) %all-gather.5.cloned.1.call-update) | async-done | bytes 1048592 | tf_op jit(solution)/shard_map/all_gather | solution.py:88
  88.6 1.1 bitcast_dynamic-update-slice_fusion.3
  89.6 1.0 bitcast_dynamic-update-slice_fusion.2
  90.6 1.0 bitcast_dynamic-update-slice_fusion.1
  91.6 1.0 bitcast_dynamic-update-slice_fusion
  92.5 0.8 copy-done.20
  93.4 0.7 dynamic_slice.45
  96.6 0.6 gather_fusion
  97.4 0.7 fusion.190
  98.3 1.0 bitcast_dynamic-update-slice_fusion.7
  99.2 1.0 bitcast_dynamic-update-slice_fusion.6
  100.2 1.0 bitcast_dynamic-update-slice_fusion.5
  101.2 0.8 copy-done.21
  102.0 19.4 %all-gather.11.cloned.1.call-done = bf16[5,512,512]{2,1,0:T(8,128)(2,1)} async-done(((bf16[5,128,512]{2,1,0:T(8,128)(2,1)}), bf16[5,512,512]{2,1,0:T(8,128)(2,1)}) %all-gather.11.cloned.1.call-update) | async-done | bytes 2621456 | tf_op jit(solution)/shard_map/all_gather | solution.py:111
  121.4 1.9 %slice_bitcast_fusion.7 = (bf16[512,512]{1,0:T(8,128)(2,1)S(1)}, bf16[512,512]{1,0:T(8,128)(2,1)S(1)}, bf16[512,512]{1,0:T(8,128)(2,1)S(1)}, bf16[512,512]{1,0:T(8,128)(2,1)S(1)}, bf16[512,512]{1,0:T(8,128)(2,1)S(1)}) fusion(bf16[5,512,512]{2,1,0:T(8,128)(2,1)} %all-gather.11.cloned.1.call-done), kind=kLoop, calls=%fused_computation.234 | loop fusion | bytes 5242880 | tf_op jit(solution)/shard_map/squeeze | solution.py:30
  123.4 1.5 bitcast_reduce_fusion.19
  125.3 1.5 bitcast_reduce_fusion.18
  126.8 1.5 bitcast_reduce_fusion.17
  128.3 1.5 bitcast_reduce_fusion.16
  129.8 1.6 bitcast_reduce_fusion.15
  131.4 1.5 bitcast_reduce_fusion.13
  132.9 1.6 bitcast_reduce_fusion.12
  134.5 1.6 bitcast_reduce_fusion.11
  136.1 1.6 bitcast_reduce_fusion.10
  137.7 1.5 bitcast_reduce_fusion.9
  139.2 1.5 bitcast_reduce_fusion.8
  140.7 1.5 bitcast_reduce_fusion.4
  142.2 1.6 bitcast_reduce_fusion.3
  143.8 1.5 bitcast_reduce_fusion.7
  145.3 1.5 bitcast_reduce_fusion.2
  146.8 1.5 bitcast_reduce_fusion.6
  148.4 1.5 bitcast_reduce_fusion.1
  149.9 1.6 bitcast_reduce_fusion
  151.5 1.5 bitcast_reduce_fusion.5
  153.0 2.1 %slice_bitcast_fusion = (bf16[512,512]{1,0:T(8,128)(2,1)S(1)}, bf16[512,512]{1,0:T(8,128)(2,1)S(1)}, bf16[512,512]{1,0:T(8,128)(2,1)S(1)}, bf16[512,512]{1,0:T(8,128)(2,1)S(1)}, bf16[512,512]{1,0:T(8,128)(2,1)S(1)}) fusion(bf16[5,512,512]{2,1,0:T(8,128)(2,1)} %all-gather.7.cloned.1.call-done), kind=kLoop, calls=%fused_computation.227 | loop fusion | bytes 5242880 | tf_op jit(solution)/shard_map/squeeze | solution.py:61
  155.2 0.4 fusion.107
  155.7 0.8 copy-done.3
  157.2 0.5 convolution_add_fusion.15
  157.7 0.8 copy-done.16
  159.2 0.5 convolution_add_fusion.14
  159.6 0.7 copy-done.17
  161.2 0.5 convolution_add_fusion.13
  161.6 0.7 copy-done.19
  162.8 0.6 copy-done.14
  163.4 3.4 %fusion.73 = (f32[6,128]{1,0:T(8,128)S(1)}, f32[6,128]{1,0:T(8,128)S(1)}, f32[6,128]{1,0:T(8,128)S(1)}, f32[6,128]{1,0:T(8,128)S(1)}, f32[6,128]{1,0:T(8,128)S(1...) fusion(f32[512,128,6]{1,0,2:T(8,128)S(1)} %copy-done.16, ...), kind=kLoop, calls=%fused_computation.135 | loop fusion | flops 11788800 | bytes 15768064 | tf_op jit(solution)/shard_map/reduce_sum | solution.py:60
  166.8 0.5 fusion.84
  167.2 0.5 fusion.81
  168.2 0.9 copy-done.4
  170.1 0.8 copy-done.6
  172.1 0.8 copy-done.1
  174.1 0.7 copy-done.9
  174.8 0.4 convolution_add_fusion.6
  175.3 0.6 copy-done.10
  175.9 3.4 %fusion.63 = (f32[6,128]{1,0:T(8,128)S(1)}, f32[6,128]{1,0:T(8,128)S(1)}, f32[6,128]{1,0:T(8,128)S(1)}, f32[6,128]{1,0:T(8,128)S(1)}, f32[6,128]{1,0:T(8,128)S(1...) fusion(f32[512,128,6]{1,0,2:T(8,128)S(1)} %copy-done.8, ...), kind=kLoop, calls=%fused_computation.125 | loop fusion | flops 11788800 | bytes 15768064 | tf_op jit(solution)/shard_map/reduce_sum | solution.py:60
  179.3 0.4 convolution_add_fusion.5
  179.7 0.4 fusion.82
  180.5 1.2 copy.94
  (72 shorter events, 8.0 us)
Async XLA Ops:
  6.5 90.1 %copy-start = (s32[8]{0:T(128)S(1)}, s32[8]{0:T(128)}, u32[]{:S(2)}) copy-start(s32[8]{0:T(128)} %param.13) | copy-start | bytes 100
  6.5 86.9 %copy-start.23 = (s32[8]{0:T(128)S(1)}, s32[8]{0:T(128)}, u32[]{:S(2)}) copy-start(s32[8]{0:T(128)} %param.11) | copy-start | bytes 100
  6.5 88.9 %copy-start.22 = (bf16[128,3072]{1,0:T(8,128)(2,1)S(1)}, bf16[128,3072]{1,0:T(8,128)(2,1)}, u32[]{:S(2)}) copy-start(bf16[128,3072]{1,0:T(8,128)(2,1)} %param.7) | copy-start | bytes 2359300
  6.5 41.0 %all-gather.9.cloned.1.call-start = ((), (), s32[]{:S(2)}) async-start(), calls=%async_computation.2 | async-start | bytes 1179648 | tf_op jit(solution)/shard_map/all_gather | solution.py:87
  7.3 81.3 %all-gather.5.cloned.1.call-start = ((), (), s32[]{:S(2)}) async-start(), calls=%async_computation | async-start | bytes 1179648 | tf_op jit(solution)/shard_map/all_gather | solution.py:88
  8.0 113.4 %all-gather.11.cloned.1.call-start = ((), (), s32[]{:S(2)}) async-start(), calls=%async_computation.3 | async-start | bytes 3276800 | tf_op jit(solution)/shard_map/all_gather | solution.py:111
  92.5 0.8 copy-start.20
  93.4 59.6 %all-gather.7.cloned.1.call-start = ((), (), s32[]{:S(2)}) async-start(), calls=%async_computation.1 | async-start | bytes 3276800 | tf_op jit(solution)/shard_map/all_gather | solution.py:112
  101.1 0.8 copy-start.21
  153.0 2.2 %copy-start.2 = (f32[512,128,6]{1,0,2:T(8,128)S(1)}, f32[512,128,6]{1,0,2:T(8,128)}, u32[]{:S(2)}) copy-start(f32[512,128,6]{1,0,2:T(8,128)} %get-tuple-element.99) | copy-start | bytes 4718596
  155.1 1.4 copy-start.3
  155.7 1.5 copy-start.12
  157.0 1.5 copy-start.16
  157.6 1.5 copy-start.13
  158.9 1.5 copy-start.17
  159.6 1.5 copy-start.15
  160.8 1.5 copy-start.19
  161.2 1.6 copy-start.18
  161.6 1.7 copy-start.14
  167.7 1.4 copy-start.4
  168.2 1.5 copy-start.5
  169.5 1.4 copy-start.6
  170.1 1.5 copy-start.7
  171.4 1.5 copy-start.1
  172.1 1.5 copy-start.8
  173.3 1.5 copy-start.9
  173.6 1.6 copy-start.11
  174.1 1.8 copy-start.10
Sparse Core Ops, SparseCore 0:
  9.5 37.9 all-gather.8
  49.6 38.9 all-gather.4
  93.5 27.8 all-gather.10
  122.8 25.5 all-gather.6
where the time goes:
time: 190 us; the launch traced here: 188 us
  waiting for transfers between devices  93.2 us (49%)
  matrix products  38.5 us (20%)
  local copies, waits for them, and re-layouts  20.9 us (11%)
  between operations  20.6 us (11%)
  other arithmetic  14.8 us (8%)
    all_gather x1, waiting for transfers between devices, per_device(): piece_values = lax.all_gather(values, 'span', axis=0, tiled=True)  41.1 us
    all_gather x1, waiting for transfers between devices, per_device(): piece_keys = lax.all_gather(keys, 'span', axis=0, tiled=True)  31.3 us
    dot_general x20, matrix products, slot_scores(): jnp.einsum('rgd,kd->grk', query_group, key_slot, preferred_element_type=j...  29.6 us
    all_gather x1, waiting for transfers between devices, per_device(): lax.all_gather(slot_keys, 'ctx', axis=1, tiled=True)  19.4 us
    unnamed x51, local copies, waits for them, and re-layouts  12.9 us
    dot_general x20, matrix products, weighted_sums(): jnp.einsum('grk,kd->rgd', weights.astype(jnp.bfloat16), value_group, pref...  8.92 us
    reduce_sum x2, other arithmetic, weighted_sums(): totals = totals + jnp.sum(weights, axis=-1)  6.8 us
    unnamed x5, other arithmetic  4.88 us
  transfers between devices with their start and end apart: 4, of which 3 were waited for; matrix products, arithmetic and copies ran while one was open for 21% of the time, Pallas kernels for 0%

commit v1 on v0

v1 whole, which is shorter than its diff:
```python
import functools
import math

import jax
import jax.numpy as jnp
from jax import lax
from jax.experimental import pallas as pl
from jax.experimental.pallas import tpu as pltpu
from jax.sharding import PartitionSpec as P

HQ = 24
KVH = 4
HD = 128
GROUP = HQ // KVH
LOW = -1e30


def attend_kernel(slots, pieces, valid_ref, first_ref, scale_ref, q_ref, *refs):
    kv_refs, out_ref = refs[:-1], refs[-1]
    rows = q_ref.shape[0]
    piece_rows = kv_refs[0].shape[0]
    row_ids = lax.broadcasted_iota(jnp.int32, (piece_rows, HD), 0)
    in_own = first_ref[0] == 0
    for g in range(KVH):
        keys_at = slice(g * HD, (g + 1) * HD)
        values_at = slice((KVH + g) * HD, (KVH + g + 1) * HD)
        heads = [g * GROUP + i for i in range(GROUP)]
        q = jnp.concatenate([q_ref[:, h * HD : (h + 1) * HD] for h in heads], axis=0)
        scale = jnp.concatenate([jnp.full((rows, 1), scale_ref[h], jnp.float32) for h in heads], axis=0)
        spare = jnp.where(
            in_own,
            kv_refs[0][0:1, keys_at].astype(jnp.float32),
            kv_refs[2][0:1, keys_at].astype(jnp.float32),
        )
        top = None
        for j in range(slots):
            ks, vs = [], []
            for i in range(pieces):
                at = j * pieces + i
                keep = row_ids < valid_ref[at]
                k = kv_refs[at][:, keys_at].astype(jnp.float32)
                v = kv_refs[at][:, values_at].astype(jnp.float32)
                ks.append(jnp.where(keep, k, spare).astype(jnp.bfloat16))
                ones = jnp.where(keep, 1.0, 0.0).astype(jnp.bfloat16)
                vs.append(jnp.concatenate([jnp.where(keep, v, 0.0).astype(jnp.bfloat16), ones], axis=1))
            k = jnp.concatenate(ks, axis=0)
            v = jnp.concatenate(vs, axis=0)
            s = lax.dot_general(q, k, (((1,), (1,)), ((), ())), preferred_element_type=jnp.float32)
            s = s * scale
            slot_top = jnp.max(s, axis=1, keepdims=True)
            if top is None:
                top = slot_top
                weight = jnp.exp2(s - top).astype(jnp.bfloat16)
                sums = jnp.dot(weight, v, preferred_element_type=jnp.float32)
            else:
                new_top = jnp.maximum(top, slot_top)
                weight = jnp.exp2(s - new_top).astype(jnp.bfloat16)
                sums = sums * jnp.exp2(top - new_top) + jnp.dot(weight, v, preferred_element_type=jnp.float32)
                top = new_top
        result = (sums[:, :HD] / sums[:, HD:]).astype(jnp.bfloat16)
        for i, h in enumerate(heads):
            out_ref[:, h * HD : (h + 1) * HD] = result[i * rows : (i + 1) * rows]


def attend(q, kv, valid, first, scale, slots, pieces):
    keys = slots * pieces * kv[0].shape[0]
    smem = pl.BlockSpec(memory_space=pltpu.SMEM)
    vmem = pl.BlockSpec(memory_space=pltpu.VMEM)
    return pl.pallas_call(
        functools.partial(attend_kernel, slots, pieces),
        out_shape=jax.ShapeDtypeStruct(q.shape, jnp.bfloat16),
        in_specs=[smem] * 3 + [vmem] * (1 + len(kv)),
        out_specs=vmem,
        compiler_params=pltpu.CompilerParams(vmem_limit_bytes=48 << 20),
        cost_estimate=pl.CostEstimate(
            flops=4 * q.shape[0] * keys * HQ * HD,
            bytes_accessed=4 * q.size + 2 * len(kv) * kv[0].size,
            transcendentals=q.shape[0] * HQ * keys,
        ),
    )(valid, first, scale, q, *kv)


def per_device(spans, ctx, queries, keys, values, temps, levels, ctx_list, counts):
    me = lax.axis_index("span")
    tok = lax.axis_index("ctx")
    rows = keys.shape[0]
    kv = jnp.concatenate([keys, values], axis=1)
    up = [(s, s + 2) for s in range(spans - 2)]
    across = [(s, s ^ 1) for s in range(spans)]
    other_chip = [(t, t ^ 2) for t in range(ctx)]
    other_core = [(t, t ^ 1) for t in range(ctx)]

    wanted = lax.dynamic_index_in_dim(ctx_list, me, 0, keepdims=False)
    straight, crossed = [kv], [lax.ppermute(kv, "span", across)]
    for step in range(1, spans // 2):
        straight.append(lax.ppermute(straight[-1], "span", up))
        crossed.append(lax.ppermute(straight[-1], "span", across))

    def pick(source):
        same = ((source ^ me) & 1) == 0
        back = jnp.where(same, me, me ^ 1) - source
        at = jnp.clip(back // 2, 0, spans // 2 - 1) + jnp.where(same, 0, spans // 2)
        return select(at, straight + crossed)

    def select(at, slabs):
        result = slabs[0]
        for i in range(1, len(slabs)):
            result = jnp.where(at == i, slabs[i], result)
        return result

    def spread(slab):
        far = lax.ppermute(slab, "ctx", other_chip)
        near = lax.ppermute(slab, "ctx", other_core)
        both = lax.ppermute(far, "ctx", other_core)
        return [slab, near, far, both]

    pieces = spread(kv)
    for j in range(wanted.shape[0]):
        pieces += spread(pick(jnp.maximum(wanted[j], 0)))

    ids = jnp.concatenate([me[None], wanted])
    lengths = jnp.where(ids >= 0, counts[jnp.maximum(ids, 0)], 0)
    starts = rows * (tok ^ jnp.arange(ctx, dtype=jnp.int32))
    valid = jnp.clip(lengths[:, None] - starts[None, :], 0, rows).reshape(-1).astype(jnp.int32)
    scale = temps[levels[me]] * (math.log2(math.e) / math.sqrt(HD))
    first = (tok & 2).reshape(1).astype(jnp.int32)
    return attend(queries, pieces, valid, first, scale, ids.shape[0], ctx)


def solution(mesh):
    return jax.shard_map(
        functools.partial(per_device, mesh.shape["span"], mesh.shape["ctx"]),
        mesh=mesh,
        in_specs=(
            P(("span", "ctx"), None),
            P(("span", "ctx"), None),
            P(("span", "ctx"), None),
            P(),
            P(),
            P(),
            P(),
        ),
        out_specs=P(("span", "ctx"), None),
        check_vma=False,
    )
```

time: 190 us -> 87.1 us (0.46)
  the two profiles are of different devices: /device:TPU:25 before, /device:TPU:0 now
where the time goes in v1:
time: 87.1 us; the launch traced here: 86.7 us
  waiting for transfers between devices  36.8 us (42%)
  starting transfers between devices  25.9 us (30%)
  Pallas kernels  12.6 us (14%)
  local copies, waits for them, and re-layouts  5.05 us (6%)
  between operations  4.83 us (6%)
  other arithmetic  1.57 us (2%)
    ppermute x3, starting transfers between devices, per_device(): straight.append(lax.ppermute(straight[-1], 'span', up))  13.7 us
    ppermute x5, waiting for transfers between devices, spread(): far = lax.ppermute(slab, 'ctx', other_chip)  13.5 us
    ppermute x3, waiting for transfers between devices, per_device(): crossed.append(lax.ppermute(straight[-1], 'span', across))  12.7 us
    pallas_call x1, Pallas kernels, attend(): pl.pallas_call(functools.partial(attend_kernel, slots, pieces), out_shape...  12.6 us
    ppermute x3, waiting for transfers between devices, per_device(): straight.append(lax.ppermute(straight[-1], 'span', up))  10.2 us
    ppermute x5, starting transfers between devices, spread(): far = lax.ppermute(slab, 'ctx', other_chip)  6.09 us
    unnamed x31, local copies, waits for them, and re-layouts  2.96 us
    ppermute x3, starting transfers between devices, per_device(): crossed.append(lax.ppermute(straight[-1], 'span', across))  2.62 us
  transfers between devices with their start and end apart: 22, of which 10 were waited for; matrix products, arithmetic and copies ran while one was open for 4% of the time, Pallas kernels for 0%

profile of v1, /device:TPU:0, one launch (start us, length us, event | category | flops | bytes accessed | tf_op | source)
XLA Modules:
  0.0 86.7 jit_solution(9415534689170604750)
XLA Ops:
  0.0 0.9 %constant_dynamic-update-slice_fusion.1 = bf16[128,1024]{1,0:T(8,128)(2,1)S(1)} fusion(bf16[128,512]{1,0:T(8,128)(2,1)} %param.8), kind=kLoop, calls=%fused_computation.7 | loop fusion | bytes 262144
  1.0 0.0 copy-done.12
  1.0 4.9 %collective-permute-start.3 = (bf16[128,1024]{1,0:T(8,128)(2,1)S(1)}, bf16[128,1024]{1,0:T(8,128)(2,1)S(1)}, u32[]{:S(2)}, u32[]{:S(2)}) collective-permute-start(bf16[128,1024]{1,0:T(8,128)(2,1)S(1)} %constant_dynamic-update-slice_fusion.refs_0_), channel_id=1, source_target_pairs={{0,8},{4,12},{8,16},{12,20},{16,24},{20,28},{1,9},{5,13},{9,17},{1... | collective-permute-start | bytes 786440 | tf_op jit(solution)/shard_map/ppermute | solution.py:96
  5.9 5.5 %collective-permute-done.3 = bf16[128,1024]{1,0:T(8,128)(2,1)S(1)} collective-permute-done((bf16[128,1024]{1,0:T(8,128)(2,1)S(1)}, bf16[128,1024]{1,0:T(8,128)(2,1)S(1)}, u32[]{:S(2)}, u32[]{:S(2)}) %collective-permute-start.3) | collective-permute-done | bytes 262176 | tf_op jit(solution)/shard_map/ppermute | solution.py:96
  11.5 4.4 %collective-permute-start.4 = (bf16[128,1024]{1,0:T(8,128)(2,1)S(1)}, bf16[128,1024]{1,0:T(8,128)(2,1)S(1)}, u32[]{:S(2)}, u32[]{:S(2)}) collective-permute-start(bf16[128,1024]{1,0:T(8,128)(2,1)S(1)} %collective-permute-done.3), channel_id=1, source_target_pairs={{0,8},{4,12},{8,16},{12,20},{16,24},{20,28},{1,9},{5,13},{9,17},{1... | collective-permute-start | bytes 786440 | tf_op jit(solution)/shard_map/ppermute | solution.py:96
  15.9 4.7 %collective-permute-done.4 = bf16[128,1024]{1,0:T(8,128)(2,1)S(1)} collective-permute-done((bf16[128,1024]{1,0:T(8,128)(2,1)S(1)}, bf16[128,1024]{1,0:T(8,128)(2,1)S(1)}, u32[]{:S(2)}, u32[]{:S(2)}) %collective-permute-start.4) | collective-permute-done | bytes 262176 | tf_op jit(solution)/shard_map/ppermute | solution.py:96
  20.5 4.4 %collective-permute-start.5 = (bf16[128,1024]{1,0:T(8,128)(2,1)S(1)}, bf16[128,1024]{1,0:T(8,128)(2,1)S(1)}, u32[]{:S(2)}, u32[]{:S(2)}) collective-permute-start(bf16[128,1024]{1,0:T(8,128)(2,1)S(1)} %collective-permute-done.4), channel_id=1, source_target_pairs={{0,8},{4,12},{8,16},{12,20},{16,24},{20,28},{1,9},{5,13},{9,17},{1... | collective-permute-start | bytes 786440 | tf_op jit(solution)/shard_map/ppermute | solution.py:96
  24.9 1.6 %collective-permute-start.9 = (bf16[128,1024]{1,0:T(8,128)(2,1)S(1)}, bf16[128,1024]{1,0:T(8,128)(2,1)S(1)}, u32[]{:S(2)}, u32[]{:S(2)}) collective-permute-start(bf16[128,1024]{1,0:T(8,128)(2,1)S(1)} %constant_dynamic-update-slice_fusion.refs_0_), channel_id=1, source_target_pairs={{0,4},{4,0},{8,12},{12,8},{16,20},{20,16},{24,28},{28,24},{1,5},{5... | collective-permute-start | bytes 786440 | tf_op jit(solution)/shard_map/ppermute | solution.py:94
  26.5 1.5 %collective-permute-start.1 = (bf16[128,1024]{1,0:T(8,128)(2,1)S(1)}, bf16[128,1024]{1,0:T(8,128)(2,1)S(1)}, u32[]{:S(2)}, u32[]{:S(2)}) collective-permute-start(bf16[128,1024]{1,0:T(8,128)(2,1)S(1)} %constant_dynamic-update-slice_fusion.refs_0_), channel_id=1, source_target_pairs={{0,2},{1,3},{2,0},{3,1},{4,6},{5,7},{6,4},{7,5},{8,10},{9,11},{10,... | collective-permute-start | bytes 786440 | tf_op jit(solution)/shard_map/ppermute | solution.py:112
  28.0 0.7 copy-done.13
  28.7 0.2 fusion.1
  28.9 0.6 collective-permute-start.8
  29.5 1.5 %collective-permute-start.7 = (bf16[128,1024]{1,0:T(8,128)(2,1)S(1)}, bf16[128,1024]{1,0:T(8,128)(2,1)S(1)}, u32[]{:S(2)}, u32[]{:S(2)}) collective-permute-start(bf16[128,1024]{1,0:T(8,128)(2,1)S(1)} %collective-permute-done.4), channel_id=1, source_target_pairs={{0,4},{4,0},{8,12},{12,8},{16,20},{20,16},{24,28},{28,24},{1,5},{5... | collective-permute-start | bytes 786440 | tf_op jit(solution)/shard_map/ppermute | solution.py:97
  31.0 0.0 collective-permute-done.5
  31.0 0.5 collective-permute-start.6
  31.5 0.6 fusion.2
  34.8 0.1 fusion
  34.9 0.0 collective-permute-done.9
  34.9 0.1 collective-permute-start
  35.0 0.0 collective-permute-done.1.refs_2_
  35.0 0.5 collective-permute-start.2
  35.5 4.1 %collective-permute-done.8 = bf16[128,1024]{1,0:T(8,128)(2,1)S(1)} collective-permute-done((bf16[128,1024]{1,0:T(8,128)(2,1)S(1)}, bf16[128,1024]{1,0:T(8,128)(2,1)S(1)}, u32[]{:S(2)}, u32[]{:S(2)}) %collective-permute-start.8) | collective-permute-done | bytes 262176 | tf_op jit(solution)/shard_map/ppermute | solution.py:97
  39.6 5.6 %collective-permute-done.7 = bf16[128,1024]{1,0:T(8,128)(2,1)S(1)} collective-permute-done((bf16[128,1024]{1,0:T(8,128)(2,1)S(1)}, bf16[128,1024]{1,0:T(8,128)(2,1)S(1)}, u32[]{:S(2)}, u32[]{:S(2)}) %collective-permute-start.7) | collective-permute-done | bytes 262176 | tf_op jit(solution)/shard_map/ppermute | solution.py:97
  45.3 3.0 %collective-permute-done.6 = bf16[128,1024]{1,0:T(8,128)(2,1)S(1)} collective-permute-done((bf16[128,1024]{1,0:T(8,128)(2,1)S(1)}, bf16[128,1024]{1,0:T(8,128)(2,1)S(1)}, u32[]{:S(2)}, u32[]{:S(2)}) %collective-permute-start.6) | collective-permute-done | bytes 262176 | tf_op jit(solution)/shard_map/ppermute | solution.py:97
  48.2 0.1 select_select_fusion.3.refs_4_
  48.3 0.6 copy-done.10
  48.9 1.1 %collective-permute-start.11 = (bf16[128,1024]{1,0:T(8,128)(2,1)S(1)}, bf16[128,1024]{1,0:T(8,128)(2,1)S(1)}, u32[]{:S(2)}, u32[]{:S(2)}) collective-permute-start(bf16[128,1024]{1,0:T(8,128)(2,1)S(1)} %select_select_fusion.3.refs_4_), channel_id=1, source_target_pairs={{0,2},{1,3},{2,0},{3,1},{4,6},{5,7},{6,4},{7,5},{8,10},{9,11},{10,... | collective-permute-start | bytes 786440 | tf_op jit(solution)/shard_map/ppermute | solution.py:112
  50.1 0.0 collective-permute-start.10
  50.1 0.2 select_select_fusion.2.refs_8_
  50.3 1.0 %collective-permute-start.14 = (bf16[128,1024]{1,0:T(8,128)(2,1)S(1)}, bf16[128,1024]{1,0:T(8,128)(2,1)}, u32[]{:S(2)}, u32[]{:S(2)}) collective-permute-start(bf16[128,1024]{1,0:T(8,128)(2,1)S(1)} %select_select_fusion.2.refs_8_), channel_id=1, source_target_pairs={{0,2},{1,3},{2,0},{3,1},{4,6},{5,7},{6,4},{7,5},{8,10},{9,11},{10,... | collective-permute-start | bytes 786440 | tf_op jit(solution)/shard_map/ppermute | solution.py:112
  51.3 0.1 select_select_fusion.refs_16_
  51.4 0.0 copy-start.1
  51.4 0.2 select_select_fusion.1.refs_12_
  51.6 0.0 collective-permute-done.refs_1_
  51.7 0.3 collective-permute-start.13
  52.0 0.0 collective-permute-done.2.refs_3_
  52.0 1.1 %collective-permute-start.17 = (bf16[128,1024]{1,0:T(8,128)(2,1)S(1)}, bf16[128,1024]{1,0:T(8,128)(2,1)}, u32[]{:S(2)}, u32[]{:S(2)}) collective-permute-start(bf16[128,1024]{1,0:T(8,128)(2,1)S(1)} %select_select_fusion.1.refs_12_), channel_id=1, source_target_pairs={{0,2},{1,3},{2,0},{3,1},{4,6},{5,7},{6,4},{7,5},{8,10},{9,11},{10,... | collective-permute-start | bytes 786440 | tf_op jit(solution)/shard_map/ppermute | solution.py:112
  53.1 4.2 %collective-permute-done.11.refs_6_ = bf16[128,1024]{1,0:T(8,128)(2,1)S(1)} collective-permute-done((bf16[128,1024]{1,0:T(8,128)(2,1)S(1)}, bf16[128,1024]{1,0:T(8,128)(2,1)S(1)}, u32[]{:S(2)}, u32[]{:S(2)}) %collective-permute-start.11) | collective-permute-done | bytes 262176 | tf_op jit(solution)/shard_map/ppermute | solution.py:112
  57.2 0.0 collective-permute-start.16
  57.2 0.0 collective-permute-done.10.refs_5_
  57.2 1.4 %collective-permute-start.20 = (bf16[128,1024]{1,0:T(8,128)(2,1)S(1)}, bf16[128,1024]{1,0:T(8,128)(2,1)}, u32[]{:S(2)}, u32[]{:S(2)}) collective-permute-start(bf16[128,1024]{1,0:T(8,128)(2,1)S(1)} %select_select_fusion.refs_16_), channel_id=1, source_target_pairs={{0,2},{1,3},{2,0},{3,1},{4,6},{5,7},{6,4},{7,5},{8,10},{9,11},{10,... | collective-permute-start | bytes 786440 | tf_op jit(solution)/shard_map/ppermute | solution.py:112
  58.6 0.7 copy-done.14
  59.3 0.6 dynamic_slice.11
  61.1 0.6 gather_fusion
  61.8 0.1 compare_select_fusion
  61.9 1.1 %collective-permute-done.14.refs_10_ = bf16[128,1024]{1,0:T(8,128)(2,1)} collective-permute-done((bf16[128,1024]{1,0:T(8,128)(2,1)S(1)}, bf16[128,1024]{1,0:T(8,128)(2,1)}, u32[]{:S(2)}, u32[]{:S(2)}) %collective-permute-start.14) | collective-permute-done | bytes 262176 | tf_op jit(solution)/shard_map/ppermute | solution.py:112
  62.9 0.0 collective-permute-start.19
  63.0 0.0 collective-permute-done.13.refs_9_
  63.0 0.5 collective-permute-start.12
  63.5 5.1 %collective-permute-done.17.refs_14_ = bf16[128,1024]{1,0:T(8,128)(2,1)} collective-permute-done((bf16[128,1024]{1,0:T(8,128)(2,1)S(1)}, bf16[128,1024]{1,0:T(8,128)(2,1)}, u32[]{:S(2)}, u32[]{:S(2)}) %collective-permute-start.17) | collective-permute-done | bytes 262176 | tf_op jit(solution)/shard_map/ppermute | solution.py:112
  68.6 0.0 collective-permute-start.15
  68.6 0.0 collective-permute-done.16.refs_13_
  68.6 0.5 collective-permute-start.18
  69.1 3.2 %collective-permute-done.20.refs_18_ = bf16[128,1024]{1,0:T(8,128)(2,1)} collective-permute-done((bf16[128,1024]{1,0:T(8,128)(2,1)S(1)}, bf16[128,1024]{1,0:T(8,128)(2,1)}, u32[]{:S(2)}, u32[]{:S(2)}) %collective-permute-start.20) | collective-permute-done | bytes 262176 | tf_op jit(solution)/shard_map/ppermute | solution.py:112
  72.3 0.0 collective-permute-start.21
  72.3 0.1 subtract_clamp_fusion
  72.3 0.1 min.25.valid_ref
  73.1 0.7 multiply_bitcast_fusion.scale_ref
  73.8 0.0 collective-permute-done.19.refs_17_
  73.8 0.0 collective-permute-done.12.refs_7_
  73.8 0.0 collective-permute-done.15.refs_11_
  73.8 0.0 collective-permute-done.18.refs_15_
  73.8 0.3 collective-permute-done.21.refs_19_
  74.1 12.6 %shard_map.73 = bf16[128,3072]{1,0:T(8,128)(2,1)} custom-call(s32[20]{0:T(128)S(1)} %min.25.valid_ref, s32[1]{0:T(128)} %bitcast.3.first_ref, f32[24]{0:T(128)S(1)} %multiply_bitcast_fusion.scale_ref, bf16[128,3072]{1,0:T(8,128)(2,1)S(1)} %copy-done.1, bf16[128,1024]{1,0:T(8,128)(2,1)S(1)} %constant_dynamic-update-slice_fusion.refs_0_, ...), custom_call_target="tpu_custom_call" | custom-call | flops 4026531840 | bytes 6815744 | tf_op jit(solution)/shard_map/pallas_call | solution.py:69
  (28 shorter events, 0.1 us)
Async XLA Ops:
  0.0 61.1 %copy-start = (s32[8]{0:T(128)S(1)}, s32[8]{0:T(128)}, u32[]{:S(2)}) copy-start(s32[8]{0:T(128)} %param.13) | copy-start | bytes 100
  0.0 1.0 %copy-start.12 = (bf16[128,512]{1,0:T(8,128)(2,1)S(1)}, bf16[128,512]{1,0:T(8,128)(2,1)}, u32[]{:S(2)}) copy-start(bf16[128,512]{1,0:T(8,128)(2,1)} %param.9) | copy-start | bytes 393220
  1.0 10.5 %collective-permute-start.3 = (bf16[128,1024]{1,0:T(8,128)(2,1)S(1)}, bf16[128,1024]{1,0:T(8,128)(2,1)S(1)}, u32[]{:S(2)}, u32[]{:S(2)}) collective-permute-start(bf16[128,1024]{1,0:T(8,128)(2,1)S(1)} %constant_dynamic-update-slice_fusion.refs_0_), channel_id=1, source_target_pairs={{0,8},{4,12},{8,16},{12,20},{16,24},{20,28},{1,9},{5,13},{9,17},{1... | collective-permute-start | bytes 786440 | tf_op jit(solution)/shard_map/ppermute | solution.py:96
  11.5 39.7 %copy-start.2 = (bf16[128,1024]{1,0:T(8,128)(2,1)}, bf16[128,1024]{1,0:T(8,128)(2,1)S(1)}, u32[]{:S(2)}) copy-start(bf16[128,1024]{1,0:T(8,128)(2,1)S(1)} %collective-permute-done.3) | copy-start | bytes 786436
  11.5 9.1 %collective-permute-start.4 = (bf16[128,1024]{1,0:T(8,128)(2,1)S(1)}, bf16[128,1024]{1,0:T(8,128)(2,1)S(1)}, u32[]{:S(2)}, u32[]{:S(2)}) collective-permute-start(bf16[128,1024]{1,0:T(8,128)(2,1)S(1)} %collective-permute-done.3), channel_id=1, source_target_pairs={{0,8},{4,12},{8,16},{12,20},{16,24},{20,28},{1,9},{5,13},{9,17},{1... | collective-permute-start | bytes 786440 | tf_op jit(solution)/shard_map/ppermute | solution.py:96
  20.5 30.7 %copy-start.3 = (bf16[128,1024]{1,0:T(8,128)(2,1)}, bf16[128,1024]{1,0:T(8,128)(2,1)S(1)}, u32[]{:S(2)}) copy-start(bf16[128,1024]{1,0:T(8,128)(2,1)S(1)} %collective-permute-done.4) | copy-start | bytes 786436
  20.5 10.4 %collective-permute-start.5 = (bf16[128,1024]{1,0:T(8,128)(2,1)S(1)}, bf16[128,1024]{1,0:T(8,128)(2,1)S(1)}, u32[]{:S(2)}, u32[]{:S(2)}) collective-permute-start(bf16[128,1024]{1,0:T(8,128)(2,1)S(1)} %collective-permute-done.4), channel_id=1, source_target_pairs={{0,8},{4,12},{8,16},{12,20},{16,24},{20,28},{1,9},{5,13},{9,17},{1... | collective-permute-start | bytes 786440 | tf_op jit(solution)/shard_map/ppermute | solution.py:96
  24.9 10.0 %collective-permute-start.9 = (bf16[128,1024]{1,0:T(8,128)(2,1)S(1)}, bf16[128,1024]{1,0:T(8,128)(2,1)S(1)}, u32[]{:S(2)}, u32[]{:S(2)}) collective-permute-start(bf16[128,1024]{1,0:T(8,128)(2,1)S(1)} %constant_dynamic-update-slice_fusion.refs_0_), channel_id=1, source_target_pairs={{0,4},{4,0},{8,12},{12,8},{16,20},{20,16},{24,28},{28,24},{1,5},{5... | collective-permute-start | bytes 786440 | tf_op jit(solution)/shard_map/ppermute | solution.py:94
  26.5 8.5 %collective-permute-start.1 = (bf16[128,1024]{1,0:T(8,128)(2,1)S(1)}, bf16[128,1024]{1,0:T(8,128)(2,1)S(1)}, u32[]{:S(2)}, u32[]{:S(2)}) collective-permute-start(bf16[128,1024]{1,0:T(8,128)(2,1)S(1)} %constant_dynamic-update-slice_fusion.refs_0_), channel_id=1, source_target_pairs={{0,2},{1,3},{2,0},{3,1},{4,6},{5,7},{6,4},{7,5},{8,10},{9,11},{10,... | collective-permute-start | bytes 786440 | tf_op jit(solution)/shard_map/ppermute | solution.py:112
  28.0 0.7 copy-start.13
  28.9 10.7 %collective-permute-start.8 = (bf16[128,1024]{1,0:T(8,128)(2,1)S(1)}, bf16[128,1024]{1,0:T(8,128)(2,1)S(1)}, u32[]{:S(2)}, u32[]{:S(2)}) collective-permute-start(bf16[128,1024]{1,0:T(8,128)(2,1)S(1)} %collective-permute-done.3), channel_id=1, source_target_pairs={{0,4},{4,0},{8,12},{12,8},{16,20},{20,16},{24,28},{28,24},{1,5},{5... | collective-permute-start | bytes 786440 | tf_op jit(solution)/shard_map/ppermute | solution.py:97
  29.5 15.8 %collective-permute-start.7 = (bf16[128,1024]{1,0:T(8,128)(2,1)S(1)}, bf16[128,1024]{1,0:T(8,128)(2,1)S(1)}, u32[]{:S(2)}, u32[]{:S(2)}) collective-permute-start(bf16[128,1024]{1,0:T(8,128)(2,1)S(1)} %collective-permute-done.4), channel_id=1, source_target_pairs={{0,4},{4,0},{8,12},{12,8},{16,20},{20,16},{24,28},{28,24},{1,5},{5... | collective-permute-start | bytes 786440 | tf_op jit(solution)/shard_map/ppermute | solution.py:97
  31.0 20.2 %copy-start.4 = (bf16[128,1024]{1,0:T(8,128)(2,1)}, bf16[128,1024]{1,0:T(8,128)(2,1)S(1)}, u32[]{:S(2)}) copy-start(bf16[128,1024]{1,0:T(8,128)(2,1)S(1)} %collective-permute-done.5) | copy-start | bytes 786436
  31.0 17.2 %collective-permute-start.6 = (bf16[128,1024]{1,0:T(8,128)(2,1)S(1)}, bf16[128,1024]{1,0:T(8,128)(2,1)S(1)}, u32[]{:S(2)}, u32[]{:S(2)}) collective-permute-start(bf16[128,1024]{1,0:T(8,128)(2,1)S(1)} %collective-permute-done.5), channel_id=1, source_target_pairs={{0,4},{4,0},{8,12},{12,8},{16,20},{20,16},{24,28},{28,24},{1,5},{5... | collective-permute-start | bytes 786440 | tf_op jit(solution)/shard_map/ppermute | solution.py:97
  34.9 16.3 %copy-start.5 = (bf16[128,1024]{1,0:T(8,128)(2,1)}, bf16[128,1024]{1,0:T(8,128)(2,1)S(1)}, u32[]{:S(2)}) copy-start(bf16[128,1024]{1,0:T(8,128)(2,1)S(1)} %collective-permute-done.9) | copy-start | bytes 786436
  34.9 16.7 %collective-permute-start = (bf16[128,1024]{1,0:T(8,128)(2,1)S(1)}, bf16[128,1024]{1,0:T(8,128)(2,1)S(1)}, u32[]{:S(2)}, u32[]{:S(2)}) collective-permute-start(bf16[128,1024]{1,0:T(8,128)(2,1)S(1)} %constant_dynamic-update-slice_fusion.refs_0_), channel_id=1, source_target_pairs={{0,1},{1,0},{2,3},{3,2},{4,5},{5,4},{6,7},{7,6},{8,9},{9,8},{10,11... | collective-permute-start | bytes 786440 | tf_op jit(solution)/shard_map/ppermute | solution.py:113
  35.0 17.0 %collective-permute-start.2 = (bf16[128,1024]{1,0:T(8,128)(2,1)S(1)}, bf16[128,1024]{1,0:T(8,128)(2,1)S(1)}, u32[]{:S(2)}, u32[]{:S(2)}) collective-permute-start(bf16[128,1024]{1,0:T(8,128)(2,1)S(1)} %collective-permute-done.1.refs_2_), channel_id=1, source_target_pairs={{0,1},{1,0},{2,3},{3,2},{4,5},{5,4},{6,7},{7,6},{8,9},{9,8},{10,11... | collective-permute-start | bytes 786440 | tf_op jit(solution)/shard_map/ppermute | solution.py:114
  39.6 10.4 %copy-start.6 = (bf16[128,1024]{1,0:T(8,128)(2,1)}, bf16[128,1024]{1,0:T(8,128)(2,1)S(1)}, u32[]{:S(2)}) copy-start(bf16[128,1024]{1,0:T(8,128)(2,1)S(1)} %collective-permute-done.8) | copy-start | bytes 786436
  45.2 3.0 %copy-start.8 = (bf16[128,1024]{1,0:T(8,128)(2,1)}, bf16[128,1024]{1,0:T(8,128)(2,1)S(1)}, u32[]{:S(2)}) copy-start(bf16[128,1024]{1,0:T(8,128)(2,1)S(1)} %collective-permute-done.7) | copy-start | bytes 786436
  48.2 0.7 copy-start.10
  48.9 2.3 %copy-start.9 = (bf16[128,1024]{1,0:T(8,128)(2,1)S(1)}, bf16[128,1024]{1,0:T(8,128)(2,1)}, u32[]{:S(2)}) copy-start(bf16[128,1024]{1,0:T(8,128)(2,1)} %copy-done.8) | copy-start | bytes 786436
  48.9 8.3 %collective-permute-start.11 = (bf16[128,1024]{1,0:T(8,128)(2,1)S(1)}, bf16[128,1024]{1,0:T(8,128)(2,1)S(1)}, u32[]{:S(2)}, u32[]{:S(2)}) collective-permute-start(bf16[128,1024]{1,0:T(8,128)(2,1)S(1)} %select_select_fusion.3.refs_4_), channel_id=1, source_target_pairs={{0,2},{1,3},{2,0},{3,1},{4,6},{5,7},{6,4},{7,5},{8,10},{9,11},{10,... | collective-permute-start | bytes 786440 | tf_op jit(solution)/shard_map/ppermute | solution.py:112
  50.1 1.2 %copy-start.11 = (bf16[128,1024]{1,0:T(8,128)(2,1)S(1)}, bf16[128,1024]{1,0:T(8,128)(2,1)}, u32[]{:S(2)}) copy-start(bf16[128,1024]{1,0:T(8,128)(2,1)} %copy-done.10) | copy-start | bytes 786436
  50.1 7.2 %collective-permute-start.10 = (bf16[128,1024]{1,0:T(8,128)(2,1)S(1)}, bf16[128,1024]{1,0:T(8,128)(2,1)S(1)}, u32[]{:S(2)}, u32[]{:S(2)}) collective-permute-start(bf16[128,1024]{1,0:T(8,128)(2,1)S(1)} %select_select_fusion.3.refs_4_), channel_id=1, source_target_pairs={{0,1},{1,0},{2,3},{3,2},{4,5},{5,4},{6,7},{7,6},{8,9},{9,8},{10,11... | collective-permute-start | bytes 786440 | tf_op jit(solution)/shard_map/ppermute | solution.py:113
  50.2 1.2 %copy-start.7 = (bf16[128,1024]{1,0:T(8,128)(2,1)S(1)}, bf16[128,1024]{1,0:T(8,128)(2,1)}, u32[]{:S(2)}) copy-start(bf16[128,1024]{1,0:T(8,128)(2,1)} %copy-done.6) | copy-start | bytes 786436
  50.3 12.7 %collective-permute-start.14 = (bf16[128,1024]{1,0:T(8,128)(2,1)S(1)}, bf16[128,1024]{1,0:T(8,128)(2,1)}, u32[]{:S(2)}, u32[]{:S(2)}) collective-permute-start(bf16[128,1024]{1,0:T(8,128)(2,1)S(1)} %select_select_fusion.2.refs_8_), channel_id=1, source_target_pairs={{0,2},{1,3},{2,0},{3,1},{4,6},{5,7},{6,4},{7,5},{8,10},{9,11},{10,... | collective-permute-start | bytes 786440 | tf_op jit(solution)/shard_map/ppermute | solution.py:112
  51.4 22.7 %copy-start.1 = (bf16[128,3072]{1,0:T(8,128)(2,1)S(1)}, bf16[128,3072]{1,0:T(8,128)(2,1)}, u32[]{:S(2)}) copy-start(bf16[128,3072]{1,0:T(8,128)(2,1)} %q_ref.1) | copy-start | bytes 2359300
  51.7 11.3 %collective-permute-start.13 = (bf16[128,1024]{1,0:T(8,128)(2,1)S(1)}, bf16[128,1024]{1,0:T(8,128)(2,1)}, u32[]{:S(2)}, u32[]{:S(2)}) collective-permute-start(bf16[128,1024]{1,0:T(8,128)(2,1)S(1)} %select_select_fusion.2.refs_8_), channel_id=1, source_target_pairs={{0,1},{1,0},{2,3},{3,2},{4,5},{5,4},{6,7},{7,6},{8,9},{9,8},{10,11... | collective-permute-start | bytes 786440 | tf_op jit(solution)/shard_map/ppermute | solution.py:113
  52.0 16.6 %collective-permute-start.17 = (bf16[128,1024]{1,0:T(8,128)(2,1)S(1)}, bf16[128,1024]{1,0:T(8,128)(2,1)}, u32[]{:S(2)}, u32[]{:S(2)}) collective-permute-start(bf16[128,1024]{1,0:T(8,128)(2,1)S(1)} %select_select_fusion.1.refs_12_), channel_id=1, source_target_pairs={{0,2},{1,3},{2,0},{3,1},{4,6},{5,7},{6,4},{7,5},{8,10},{9,11},{10,... | collective-permute-start | bytes 786440 | tf_op jit(solution)/shard_map/ppermute | solution.py:112
  57.2 11.3 %collective-permute-start.16 = (bf16[128,1024]{1,0:T(8,128)(2,1)S(1)}, bf16[128,1024]{1,0:T(8,128)(2,1)}, u32[]{:S(2)}, u32[]{:S(2)}) collective-permute-start(bf16[128,1024]{1,0:T(8,128)(2,1)S(1)} %select_select_fusion.1.refs_12_), channel_id=1, source_target_pairs={{0,1},{1,0},{2,3},{3,2},{4,5},{5,4},{6,7},{7,6},{8,9},{9,8},{10,11... | collective-permute-start | bytes 786440 | tf_op jit(solution)/shard_map/ppermute | solution.py:113
  57.2 15.0 %collective-permute-start.20 = (bf16[128,1024]{1,0:T(8,128)(2,1)S(1)}, bf16[128,1024]{1,0:T(8,128)(2,1)}, u32[]{:S(2)}, u32[]{:S(2)}) collective-permute-start(bf16[128,1024]{1,0:T(8,128)(2,1)S(1)} %select_select_fusion.refs_16_), channel_id=1, source_target_pairs={{0,2},{1,3},{2,0},{3,1},{4,6},{5,7},{6,4},{7,5},{8,10},{9,11},{10,... | collective-permute-start | bytes 786440 | tf_op jit(solution)/shard_map/ppermute | solution.py:112
  58.6 0.7 copy-start.14
  62.9 10.8 %collective-permute-start.19 = (bf16[128,1024]{1,0:T(8,128)(2,1)S(1)}, bf16[128,1024]{1,0:T(8,128)(2,1)}, u32[]{:S(2)}, u32[]{:S(2)}) collective-permute-start(bf16[128,1024]{1,0:T(8,128)(2,1)S(1)} %select_select_fusion.refs_16_), channel_id=1, source_target_pairs={{0,1},{1,0},{2,3},{3,2},{4,5},{5,4},{6,7},{7,6},{8,9},{9,8},{10,11... | collective-permute-start | bytes 786440 | tf_op jit(solution)/shard_map/ppermute | solution.py:113
  63.0 10.8 %collective-permute-start.12 = (bf16[128,1024]{1,0:T(8,128)(2,1)S(1)}, bf16[128,1024]{1,0:T(8,128)(2,1)}, u32[]{:S(2)}, u32[]{:S(2)}) collective-permute-start(bf16[128,1024]{1,0:T(8,128)(2,1)S(1)} %collective-permute-done.11.refs_6_), channel_id=1, source_target_pairs={{0,1},{1,0},{2,3},{3,2},{4,5},{5,4},{6,7},{7,6},{8,9},{9,8},{10,11... | collective-permute-start | bytes 786440 | tf_op jit(solution)/shard_map/ppermute | solution.py:114
  68.6 5.2 %collective-permute-start.15 = (bf16[128,1024]{1,0:T(8,128)(2,1)}, bf16[128,1024]{1,0:T(8,128)(2,1)}, u32[]{:S(2)}, u32[]{:S(2)}) collective-permute-start(bf16[128,1024]{1,0:T(8,128)(2,1)} %collective-permute-done.14.refs_10_), channel_id=1, source_target_pairs={{0,1},{1,0},{2,3},{3,2},{4,5},{5,4},{6,7},{7,6},{8,9},{9,8},{10,11... | collective-permute-start | bytes 786440 | tf_op jit(solution)/shard_map/ppermute | solution.py:114
  68.6 5.2 %collective-permute-start.18 = (bf16[128,1024]{1,0:T(8,128)(2,1)}, bf16[128,1024]{1,0:T(8,128)(2,1)}, u32[]{:S(2)}, u32[]{:S(2)}) collective-permute-start(bf16[128,1024]{1,0:T(8,128)(2,1)} %collective-permute-done.17.refs_14_), channel_id=1, source_target_pairs={{0,1},{1,0},{2,3},{3,2},{4,5},{5,4},{6,7},{7,6},{8,9},{9,8},{10,11... | collective-permute-start | bytes 786440 | tf_op jit(solution)/shard_map/ppermute | solution.py:114
  72.3 1.9 %collective-permute-start.21 = (bf16[128,1024]{1,0:T(8,128)(2,1)}, bf16[128,1024]{1,0:T(8,128)(2,1)}, u32[]{:S(2)}, u32[]{:S(2)}) collective-permute-start(bf16[128,1024]{1,0:T(8,128)(2,1)} %collective-permute-done.20.refs_18_), channel_id=1, source_target_pairs={{0,1},{1,0},{2,3},{3,2},{4,5},{5,4},{6,7},{7,6},{8,9},{9,8},{10,11... | collective-permute-start | bytes 786440 | tf_op jit(solution)/shard_map/ppermute | solution.py:114

commit v2 on v1

v2 whole, which is shorter than its diff:
```python
import functools
import math

import jax
import jax.numpy as jnp
from jax import lax
from jax.experimental import pallas as pl
from jax.experimental.pallas import tpu as pltpu
from jax.sharding import PartitionSpec as P

HQ = 24
KVH = 4
HD = 128
GROUP = HQ // KVH
WIDE = GROUP * HD
SCALE = math.log2(math.e) / math.sqrt(HD)
SMEM = pl.BlockSpec(memory_space=pltpu.SMEM)
ANY = pl.BlockSpec(memory_space=pl.ANY)
PARAMS = pltpu.CompilerParams(vmem_limit_bytes=40 << 20)


def plan_kernel(ready, where_ref, list_ref, counts_ref, pick_ref, count_ref):
    span = where_ref[0]
    slots = []
    for j in range(list_ref.shape[1]):
        ident = list_ref[span, j]
        other = (ident ^ span) & 1
        back = ((span ^ other) - ident) >> 1
        slots.append([ident, 2 * back + other, back + 1 + other, ident < 0])
    count_ref[0] = counts_ref[span]
    for lane, turn in enumerate(ready):
        free = jnp.bool_(True)
        pick = jnp.int32(0)
        count = jnp.int32(0)
        for slot in slots:
            ident, number, at, done = slot
            take = free & (at <= turn) & jnp.logical_not(done)
            pick = jnp.where(take, number, pick)
            count = jnp.where(take, counts_ref[jnp.maximum(ident, 0)], count)
            slot[3] = done | take
            free = free & jnp.logical_not(take)
        pick_ref[lane] = pick
        count_ref[lane + 1] = count


def plan(where, ctx_list, counts, ready):
    return pl.pallas_call(
        functools.partial(plan_kernel, ready),
        out_shape=[
            jax.ShapeDtypeStruct((len(ready),), jnp.int32),
            jax.ShapeDtypeStruct((len(ready) + 1,), jnp.int32),
        ],
        in_specs=[SMEM] * 3,
        out_specs=[SMEM] * 2,
    )(where, ctx_list, counts)


def pick_kernel(lane, numbers, pick_ref, *refs):
    slabs, out_ref, sem = refs[:-2], refs[-2], refs[-1]
    wanted = pick_ref[lane]
    known = functools.reduce(jnp.logical_or, [wanted == n for n in numbers[1:]], jnp.bool_(False))
    for i, (number, slab) in enumerate(zip(numbers, slabs)):

        @pl.when(jnp.logical_not(known) if i == 0 else wanted == number)
        def _():
            copy = pltpu.make_async_copy(slab, out_ref, sem)
            copy.start()
            copy.wait()


def pick_slab(picks, lane, slabs):
    numbers = sorted(slabs)
    return pl.pallas_call(
        functools.partial(pick_kernel, lane, numbers),
        out_shape=jax.ShapeDtypeStruct(slabs[numbers[0]].shape, jnp.bfloat16),
        in_specs=[SMEM] + [ANY] * len(numbers),
        out_specs=ANY,
        scratch_shapes=[pltpu.SemaphoreType.DMA],
    )(picks, *[slabs[n] for n in numbers])


def attend_kernel(lanes, first, final, where_ref, levels_ref, temps_ref, count_ref, q_ref, *refs):
    refs = list(refs)
    state_in = None if first else (refs.pop(0), refs.pop(0))
    pieces = [[(refs.pop(0), refs.pop(0)) for _ in range(KVH)] for _ in lanes]
    outs = [refs.pop(0)] if final else [refs.pop(0), refs.pop(0)]
    sums_ref, top_ref = refs
    rows = q_ref.shape[0]
    tall = GROUP * rows
    tok = where_ref[1]
    level = levels_ref[where_ref[0]]
    head = pl.program_id(0) * GROUP
    factors = [temps_ref[level, head + i] * SCALE for i in range(GROUP)]
    row_ids = lax.broadcasted_iota(jnp.int32, (rows, HD), 0)

    def visit(lane, count, fresh):
        lane = pieces[lane]
        low = tok < 2
        spare = jnp.where(low, lane[0][0][0:16].astype(jnp.float32), lane[2][0][0:16].astype(jnp.float32))[0:1]
        ks, vs = [], []
        for i, (k_ref, v_ref) in enumerate(lane):
            keep = row_ids < count - rows * (tok ^ i)
            ks.append(jnp.where(keep, k_ref[...].astype(jnp.float32), spare).astype(jnp.bfloat16))
            v = jnp.where(keep, v_ref[...].astype(jnp.float32), 0.0).astype(jnp.bfloat16)
            vs.append(jnp.concatenate([v, jnp.where(keep, 1.0, 0.0).astype(jnp.bfloat16)], axis=1))
        k = jnp.concatenate(ks, axis=0)
        v = jnp.concatenate(vs, axis=0)
        q = jnp.concatenate([q_ref[:, i * HD : (i + 1) * HD] for i in range(GROUP)], axis=0)
        scale = jnp.concatenate([jnp.full((rows, 1), f, jnp.float32) for f in factors], axis=0)
        s = lax.dot_general(q, k, (((1,), (1,)), ((), ())), preferred_element_type=jnp.float32)
        s = s * scale
        top = jnp.max(s, axis=1, keepdims=True)
        if not fresh:
            old_top = top_ref[:, 0:1]
            top = jnp.maximum(top, old_top)
        weight = jnp.exp2(s - top).astype(jnp.bfloat16)
        sums = jnp.dot(weight, v, preferred_element_type=jnp.float32)
        if not fresh:
            sums = sums + sums_ref[...] * jnp.exp2(old_top - top)
        sums_ref[...] = sums
        top_ref[...] = jnp.broadcast_to(top, (tall, HD))

    if not first:
        sums_in, stats_in = state_in
        sums_ref[:, :HD] = sums_in[0]
        sums_ref[:, HD:] = jnp.broadcast_to(stats_in[0, :, HD // 2 : HD // 2 + 1], (tall, HD))
        top_ref[...] = jnp.broadcast_to(stats_in[0, :, 0:1], (tall, HD))
    for i, lane in enumerate(lanes):
        count = count_ref[lane]
        if lane == 0:
            visit(i, count, True)
        else:
            pl.when(count > 0)(functools.partial(visit, i, count, False))
    if final:
        result = (sums_ref[:, :HD] / sums_ref[:, HD:]).astype(jnp.bfloat16)
        for i in range(GROUP):
            outs[0][:, i * HD : (i + 1) * HD] = result[i * rows : (i + 1) * rows]
    else:
        lane_ids = lax.broadcasted_iota(jnp.int32, (tall, HD), 1)
        outs[0][0] = sums_ref[:, :HD]
        outs[1][0] = jnp.where(lane_ids < HD // 2, top_ref[...], sums_ref[:, HD:])


def attend(scalars, q, state, pieces, lanes, final):
    rows = q.shape[0]
    tall = GROUP * rows
    state_spec = pl.BlockSpec((1, tall, HD), lambda g: (g, 0, 0))
    q_spec = pl.BlockSpec((rows, WIDE), lambda g: (0, g))
    piece_specs = [pl.BlockSpec((rows, HD), lambda g: (0, g)), pl.BlockSpec((rows, HD), lambda g: (0, g + KVH))]
    flat = [p for lane in lanes for p in pieces[lane]]
    if final:
        out_shape = jax.ShapeDtypeStruct(q.shape, jnp.bfloat16)
        out_specs = q_spec
    else:
        out_shape = [jax.ShapeDtypeStruct((KVH, tall, HD), jnp.float32)] * 2
        out_specs = [state_spec] * 2
    keys = len(flat) * rows
    return pl.pallas_call(
        functools.partial(attend_kernel, lanes, state is None, final),
        grid=(KVH,),
        out_shape=out_shape,
        in_specs=[SMEM] * 4 + [q_spec] + ([] if state is None else [state_spec] * 2) + piece_specs * len(flat),
        out_specs=out_specs,
        scratch_shapes=[pltpu.VMEM((tall, 2 * HD), jnp.float32), pltpu.VMEM((tall, HD), jnp.float32)],
        compiler_params=PARAMS,
        cost_estimate=pl.CostEstimate(
            flops=4 * KVH * tall * keys * HD,
            bytes_accessed=2 * q.size + 4 * keys * KVH * HD,
            transcendentals=KVH * tall * keys,
        ),
    )(*scalars, q, *(state or ()), *[p for piece in flat for p in (piece, piece)])


def per_device(spans, ctx, queries, keys, values, temps, levels, ctx_list, counts):
    where = jnp.stack([lax.axis_index("span"), lax.axis_index("ctx")]).astype(jnp.int32)
    turns = spans // 2
    ready = list(range(2, turns + 1)) + [turns, turns + 1]
    picks, lane_counts = plan(where, ctx_list, counts, ready)
    kv = jnp.concatenate([keys, values], axis=1)
    up = [(s, (s + 2) % spans) for s in range(spans)]
    across = [(s, s ^ 1) for s in range(spans)]
    other_chip = [(t, t ^ 2) for t in range(ctx)]
    other_core = [(t, t ^ 1) for t in range(ctx)]

    def near(slab):
        return lax.ppermute(slab, "ctx", other_core)

    slabs = {0: kv}
    lanes = []
    for turn in range(1, turns + 2):
        held = dict(slabs)
        if turn < turns:
            slabs[2 * turn] = lax.ppermute(held[2 * turn - 2], "span", up)
        if turn <= turns:
            slabs[2 * turn - 1] = lax.ppermute(held[2 * turn - 2], "span", across)
        for lane in lanes:
            if len(lane) == 3:
                lane.append(near(lane[2]))
        if turn == 1:
            leave = [kv]
        else:
            leave = [pick_slab(picks, i, held) for i, at in enumerate(ready) if at == turn]
        for slab in leave:
            lanes.append([slab, near(slab), lax.ppermute(slab, "ctx", other_chip)])
        if turn <= turns:
            slabs, lanes = lax.optimization_barrier((slabs, lanes))
    for lane in lanes:
        if len(lane) == 3:
            lane.append(near(lane[2]))

    scalars = (where, levels, temps, lane_counts)
    total = len(lanes)
    stages = [list(range(total - 3)), [total - 3, total - 2], [total - 1]]
    state = None
    for stage in stages[:-1]:
        state = attend(scalars, queries, state, lanes, stage, False)
    return attend(scalars, queries, state, lanes, stages[-1], True)


def solution(mesh):
    return jax.shard_map(
        functools.partial(per_device, mesh.shape["span"], mesh.shape["ctx"]),
        mesh=mesh,
        in_specs=(
            P(("span", "ctx"), None),
            P(("span", "ctx"), None),
            P(("span", "ctx"), None),
            P(),
            P(),
            P(),
            P(),
        ),
        out_specs=P(("span", "ctx"), None),
        check_vma=False,
    )
```

time: 87.1 us -> 152 us (1.75)
  the two profiles are of different devices: /device:TPU:0 before, /device:TPU:25 now
where the time goes in v2:
time: 152 us; the launch traced here: 150 us
  Pallas kernels  86 us (57%)
  waiting for transfers between devices  25.4 us (17%)
  starting transfers between devices  24.5 us (16%)
  local copies, waits for them, and re-layouts  13.5 us (9%)
    pallas_call x5, Pallas kernels, pick_slab(): pl.pallas_call(functools.partial(pick_kernel, lane, numbers), out_shape=j...  48.6 us
    pallas_call x3, Pallas kernels, attend(): pl.pallas_call(functools.partial(attend_kernel, lanes, state is None, fin...  36 us
    ppermute x6, waiting for transfers between devices, per_device(): lanes.append([slab, near(slab), lax.ppermute(slab, 'ctx', other_chip)])  13.3 us
    unnamed x66, local copies, waits for them, and re-layouts  12.6 us
    ppermute x12, starting transfers between devices, near(): return lax.ppermute(slab, 'ctx', other_core)  10.3 us
    ppermute x3, waiting for transfers between devices, per_device(): slabs[2 * turn] = lax.ppermute(held[2 * turn - 2], 'span', up)  8.05 us
    ppermute x6, starting transfers between devices, per_device(): lanes.append([slab, near(slab), lax.ppermute(slab, 'ctx', other_chip)])  5.02 us
    ppermute x4, starting transfers between devices, per_device(): slabs[2 * turn - 1] = lax.ppermute(held[2 * turn - 2], 'span', across)  4.84 us
  transfers between devices with their start and end apart: 25, of which 10 were waited for; matrix products, arithmetic and copies ran while one was open for 1% of the time, Pallas kernels for 25%

profile of v2, /device:TPU:25, one launch (start us, length us, event | category | flops | bytes accessed | tf_op | source)
XLA Modules:
  0.0 150.3 jit_solution(12662698326396823653)
XLA Ops:
  0.0 0.9 constant_dynamic-update-slice_fusion.1
  0.9 0.9 constant_dynamic-update-slice_fusion.refs_0_.refs_1_
  1.8 0.0 copy-start
  1.8 1.3 collective-permute-start.3
  3.2 1.0 collective-permute-start.2
  4.1 1.2 collective-permute-start
  5.3 1.3 copy.8.list_ref
  6.7 0.6 pad_add_fusion.where_ref
  7.3 1.4 shard_map.73
  8.6 0.5 collective-permute-done.3.refs_4_.refs_5_
  9.1 3.0 %collective-permute-done.1.refs_2_ = bf16[128,1024]{1,0:T(8,128)(2,1)S(1)} collective-permute-done((bf16[128,1024]{1,0:T(8,128)(2,1)S(1)}, bf16[128,1024]{1,0:T(8,128)(2,1)S(1)}, u32[]{:S(2)}, u32[]{:S(2)}) %collective-permute-start.1) | collective-permute-done | bytes 262176 | tf_op jit(solution)/shard_map/ppermute | solution.py:193
  12.0 0.0 collective-permute-done.refs_1_
  12.1 0.7 copy-done.26
  12.8 0.1 copy-done.27
  12.9 9.7 %shard_map.74.refs_8_.refs_9_ = bf16[128,1024]{1,0:T(8,128)(2,1)} custom-call(s32[5]{0:T(128)} %get-tuple-element.80.pick_ref, bf16[128,1024]{1,0:T(8,128)(2,1)} %copy-done, bf16[128,1024]{1,0:T(8,128)(2,1)} %copy-done.27, bf16[128,1024]{1,0:T(8,128)(2,1)} %copy-done.26), custom_call_target="tpu_custom_call" | custom-call | tf_op jit(solution)/shard_map/pallas_call | solution.py:73
  22.6 0.3 collective-permute-start.8
  22.9 1.1 collective-permute-start.7
  23.9 0.0 collective-permute-start.6
  23.9 1.8 %collective-permute-start.5 = (bf16[128,1024]{1,0:T(8,128)(2,1)}, bf16[128,1024]{1,0:T(8,128)(2,1)S(1)}, u32[]{:S(2)}, u32[]{:S(2)}) collective-permute-start(bf16[128,1024]{1,0:T(8,128)(2,1)} %copy-done.26), channel_id=1, source_target_pairs={{0,8},{4,12},{8,16},{12,20},{16,24},{20,28},{24,0},{28,4},{1,9},{5... | collective-permute-start | bytes 786440 | tf_op jit(solution)/shard_map/ppermute | solution.py:193
  25.7 1.2 collective-permute-start.4
  27.0 2.9 %collective-permute-done.8.refs_12_.refs_13_ = bf16[128,1024]{1,0:T(8,128)(2,1)S(1)} collective-permute-done((bf16[128,1024]{1,0:T(8,128)(2,1)}, bf16[128,1024]{1,0:T(8,128)(2,1)S(1)}, u32[]{:S(2)}, u32[]{:S(2)}) %collective-permute-start.8) | collective-permute-done | bytes 262176 | tf_op jit(solution)/shard_map/ppermute | solution.py:204
  29.9 1.6 %collective-permute-done.5.refs_4_ = bf16[128,1024]{1,0:T(8,128)(2,1)S(1)} collective-permute-done((bf16[128,1024]{1,0:T(8,128)(2,1)}, bf16[128,1024]{1,0:T(8,128)(2,1)S(1)}, u32[]{:S(2)}, u32[]{:S(2)}) %collective-permute-start.5) | collective-permute-done | bytes 262176 | tf_op jit(solution)/shard_map/ppermute | solution.py:193
  31.5 1.5 collective-permute-done.4.refs_3_
  33.0 0.7 copy-done.29
  33.7 9.7 %shard_map.75.refs_16_.refs_17_ = bf16[128,1024]{1,0:T(8,128)(2,1)} custom-call(s32[5]{0:T(128)} %get-tuple-element.80.pick_ref, bf16[128,1024]{1,0:T(8,128)(2,1)} %copy-done, bf16[128,1024]{1,0:T(8,128)(2,1)} %copy-done.27, bf16[128,1024]{1,0:T(8,128)(2,1)} %copy-done.26, bf16[128,1024]{1,0:T(8,128)(2,1)} %copy-done.29, bf16[128,1024]{1,0:T(8,128)(2,1)} %copy-done.28), custom_call_target="tpu_custom_call" | custom-call | tf_op jit(solution)/shard_map/pallas_call | solution.py:73
  43.4 1.3 collective-permute-start.13
  44.7 2.0 %collective-permute-start.12 = (bf16[128,1024]{1,0:T(8,128)(2,1)}, bf16[128,1024]{1,0:T(8,128)(2,1)S(1)}, u32[]{:S(2)}, u32[]{:S(2)}) collective-permute-start(bf16[128,1024]{1,0:T(8,128)(2,1)} %shard_map.75.refs_16_.refs_17_), channel_id=1, source_target_pairs={{0,1},{1,0},{2,3},{3,2},{4,5},{5,4},{6,7},{7,6},{8,9},{9,8},{10,11... | collective-permute-start | bytes 786440 | tf_op jit(solution)/shard_map/ppermute | solution.py:186
  46.7 2.5 %collective-permute-start.10 = (bf16[128,1024]{1,0:T(8,128)(2,1)}, bf16[128,1024]{1,0:T(8,128)(2,1)S(1)}, u32[]{:S(2)}, u32[]{:S(2)}) collective-permute-start(bf16[128,1024]{1,0:T(8,128)(2,1)} %copy-done.28), channel_id=1, source_target_pairs={{0,8},{4,12},{8,16},{12,20},{16,24},{20,28},{24,0},{28,4},{1,9},{5... | collective-permute-start | bytes 786440 | tf_op jit(solution)/shard_map/ppermute | solution.py:193
  49.2 1.2 collective-permute-start.9
  50.4 0.7 copy-done.20
  51.2 3.5 %collective-permute-done.10.refs_6_ = bf16[128,1024]{1,0:T(8,128)(2,1)S(1)} collective-permute-done((bf16[128,1024]{1,0:T(8,128)(2,1)}, bf16[128,1024]{1,0:T(8,128)(2,1)S(1)}, u32[]{:S(2)}, u32[]{:S(2)}) %collective-permute-start.10) | collective-permute-done | bytes 262176 | tf_op jit(solution)/shard_map/ppermute | solution.py:193
  54.7 1.8 %collective-permute-done.9.refs_5_ = bf16[128,1024]{1,0:T(8,128)(2,1)S(1)} collective-permute-done((bf16[128,1024]{1,0:T(8,128)(2,1)}, bf16[128,1024]{1,0:T(8,128)(2,1)S(1)}, u32[]{:S(2)}, u32[]{:S(2)}) %collective-permute-start.9) | collective-permute-done | bytes 262176 | tf_op jit(solution)/shard_map/ppermute | solution.py:195
  56.5 0.7 copy-done.31
  57.2 9.7 %shard_map.76.refs_2_.refs_3_ = bf16[128,1024]{1,0:T(8,128)(2,1)} custom-call(s32[5]{0:T(128)} %get-tuple-element.80.pick_ref, bf16[128,1024]{1,0:T(8,128)(2,1)} %copy-done, bf16[128,1024]{1,0:T(8,128)(2,1)} %copy-done.27, bf16[128,1024]{1,0:T(8,128)(2,1)} %copy-done.26, bf16[128,1024]{1,0:T(8,128)(2,1)} %copy-done.29, bf16[128,1024]{1,0:T(8,128)(2,1)} %copy-done.28, ...), custom_call_target="tpu_custom_call" | custom-call | tf_op jit(solution)/shard_map/pallas_call | solution.py:73
  66.9 0.3 collective-permute-start.17
  67.2 9.7 %shard_map.77.refs_10_.refs_11_ = bf16[128,1024]{1,0:T(8,128)(2,1)} custom-call(s32[5]{0:T(128)} %get-tuple-element.80.pick_ref, bf16[128,1024]{1,0:T(8,128)(2,1)} %copy-done, bf16[128,1024]{1,0:T(8,128)(2,1)} %copy-done.27, bf16[128,1024]{1,0:T(8,128)(2,1)} %copy-done.26, bf16[128,1024]{1,0:T(8,128)(2,1)} %copy-done.29, bf16[128,1024]{1,0:T(8,128)(2,1)} %copy-done.28, ...), custom_call_target="tpu_custom_call" | custom-call | tf_op jit(solution)/shard_map/pallas_call | solution.py:73
  77.0 0.0 copy-start.1
  77.0 0.0 copy-start.2
  77.0 0.0 copy-start.8
  77.0 0.0 copy-start.10
  77.1 2.0 %collective-permute-start.16 = (bf16[128,1024]{1,0:T(8,128)(2,1)S(1)}, bf16[128,1024]{1,0:T(8,128)(2,1)S(1)}, u32[]{:S(2)}, u32[]{:S(2)}) collective-permute-start(bf16[128,1024]{1,0:T(8,128)(2,1)S(1)} %copy-done.3), channel_id=1, source_target_pairs={{0,1},{1,0},{2,3},{3,2},{4,5},{5,4},{6,7},{7,6},{8,9},{9,8},{10,11... | collective-permute-start | bytes 786440 | tf_op jit(solution)/shard_map/ppermute | solution.py:186
  79.1 1.3 collective-permute-start.19
  80.3 0.3 collective-permute-start.18
  80.7 0.2 collective-permute-start.15
  80.9 1.2 collective-permute-start.14
  82.1 5.2 %collective-permute-done.19.refs_14_.refs_15_ = bf16[128,1024]{1,0:T(8,128)(2,1)S(1)} collective-permute-done((bf16[128,1024]{1,0:T(8,128)(2,1)}, bf16[128,1024]{1,0:T(8,128)(2,1)S(1)}, u32[]{:S(2)}, u32[]{:S(2)}) %collective-permute-start.19) | collective-permute-done | bytes 262176 | tf_op jit(solution)/shard_map/ppermute | solution.py:204
  87.3 0.7 copy-done.24
  88.0 0.7 collective-permute-done.14.refs_7_
  88.7 9.7 %shard_map.80.refs_2_.refs_3_ = bf16[128,1024]{1,0:T(8,128)(2,1)} custom-call(s32[5]{0:T(128)} %get-tuple-element.80.pick_ref, bf16[128,1024]{1,0:T(8,128)(2,1)} %copy-done, bf16[128,1024]{1,0:T(8,128)(2,1)} %copy-done.27, bf16[128,1024]{1,0:T(8,128)(2,1)} %copy-done.26, bf16[128,1024]{1,0:T(8,128)(2,1)} %copy-done.29, bf16[128,1024]{1,0:T(8,128)(2,1)} %copy-done.28, ...), custom_call_target="tpu_custom_call" | custom-call | tf_op jit(solution)/shard_map/pallas_call | solution.py:73
  98.5 0.6 collective-permute-start.23
  99.0 1.2 collective-permute-start.20
  100.2 0.5 collective-permute-start.22
  100.7 4.6 %collective-permute-done.23.refs_6_.refs_7_ = bf16[128,1024]{1,0:T(8,128)(2,1)S(1)} collective-permute-done((bf16[128,1024]{1,0:T(8,128)(2,1)}, bf16[128,1024]{1,0:T(8,128)(2,1)S(1)}, u32[]{:S(2)}, u32[]{:S(2)}) %collective-permute-start.23) | collective-permute-done | bytes 262176 | tf_op jit(solution)/shard_map/ppermute | solution.py:204
  105.4 2.1 %collective-permute-start.24 = (bf16[128,1024]{1,0:T(8,128)(2,1)S(1)}, bf16[128,1024]{1,0:T(8,128)(2,1)S(1)}, u32[]{:S(2)}, u32[]{:S(2)}) collective-permute-start(bf16[128,1024]{1,0:T(8,128)(2,1)S(1)} %collective-permute-done.23.refs_6_.refs_7_), channel_id=1, source_target_pairs={{0,1},{1,0},{2,3},{3,2},{4,5},{5,4},{6,7},{7,6},{8,9},{9,8},{10,11... | collective-permute-start | bytes 786440 | tf_op jit(solution)/shard_map/ppermute | solution.py:186
  107.5 0.9 copy-done.13
  108.5 0.9 copy-done.15
  109.4 0.9 copy-done.17
  110.4 0.9 copy-done.19
  111.3 0.9 copy-done.21
  112.3 0.9 copy-done.23
  113.2 0.9 copy-done.25
  114.2 13.2 %shard_map.78 = (f32[4,768,128]{2,1,0:T(8,128)S(1)}, f32[4,768,128]{2,1,0:T(8,128)S(1)}) custom-call(s32[2]{0:T(128)S(1)} %copy-done.9, s32[8]{0:T(128)S(1)} %copy-done.10, f32[8,24]{1,0:T(8,128)S(1)} %copy-done.8, s32[6]{0:T(128)S(1)} %copy-done.11, bf16[128,3072]{1,0:T(8,128)(2,1)S(1)} %copy-done.2, bf16[128,1024]{1,0:T(8,128)(2,1)S(1)} %copy-done.1, ...), custom_call_target="tpu_custom_call" | custom-call | flops 2415919104 | bytes 3932160 | tf_op jit(solution)/shard_map/pallas_call | solution.py:158
  127.4 14.0 %shard_map.79 = (f32[4,768,128]{2,1,0:T(8,128)S(1)}, f32[4,768,128]{2,1,0:T(8,128)S(1)}) custom-call(s32[2]{0:T(128)S(1)} %copy-done.9, s32[8]{0:T(128)S(1)} %copy-done.10, f32[8,24]{1,0:T(8,128)S(1)} %copy-done.8, s32[6]{0:T(128)S(1)} %copy-done.11, bf16[128,3072]{1,0:T(8,128)(2,1)S(1)} %copy-done.2, f32[4,768,128]{2,1,0:T(8,128)S(1)} %get-tuple-element.123.refs_0_, ...), custom_call_target="tpu_custom_call" | custom-call | flops 1610612736 | bytes 2883584 | tf_op jit(solution)/shard_map/pallas_call | solution.py:158
  141.5 8.8 %shard_map.81 = bf16[128,3072]{1,0:T(8,128)(2,1)} custom-call(s32[2]{0:T(128)S(1)} %copy-done.9, s32[8]{0:T(128)S(1)} %copy-done.10, f32[8,24]{1,0:T(8,128)S(1)} %copy-done.8, s32[6]{0:T(128)S(1)} %copy-done.11, bf16[128,3072]{1,0:T(8,128)(2,1)S(1)} %copy-done.2, f32[4,768,128]{2,1,0:T(8,128)S(1)} %get-tuple-element.131.refs_0_, ...), custom_call_target="tpu_custom_call" | custom-call | flops 805306368 | bytes 1835008 | tf_op jit(solution)/shard_map/pallas_call | solution.py:158
  (63 shorter events, 0.1 us)
Async XLA Ops:
  1.8 10.2 %copy-start = (bf16[128,1024]{1,0:T(8,128)(2,1)}, bf16[128,1024]{1,0:T(8,128)(2,1)S(1)}, u32[]{:S(2)}) copy-start(bf16[128,1024]{1,0:T(8,128)(2,1)S(1)} %constant_dynamic-update-slice_fusion.refs_0_.refs_1_) | copy-start | bytes 786436
  1.8 7.2 %collective-permute-start.3 = (bf16[128,1024]{1,0:T(8,128)(2,1)S(1)}, bf16[128,1024]{1,0:T(8,128)(2,1)S(1)}, u32[]{:S(2)}, u32[]{:S(2)}) collective-permute-start(bf16[128,1024]{1,0:T(8,128)(2,1)S(1)} %constant_dynamic-update-slice_fusion.refs_0_.refs_1_), channel_id=1, source_target_pairs={{0,2},{1,3},{2,0},{3,1},{4,6},{5,7},{6,4},{7,5},{8,10},{9,11},{10,... | collective-permute-start | bytes 786440 | tf_op jit(solution)/shard_map/ppermute | solution.py:204
  3.2 5.9 %collective-permute-start.2 = (bf16[128,1024]{1,0:T(8,128)(2,1)S(1)}, bf16[128,1024]{1,0:T(8,128)(2,1)S(1)}, u32[]{:S(2)}, u32[]{:S(2)}) collective-permute-start(bf16[128,1024]{1,0:T(8,128)(2,1)S(1)} %constant_dynamic-update-slice_fusion.refs_0_.refs_1_), channel_id=1, source_target_pairs={{0,1},{1,0},{2,3},{3,2},{4,5},{5,4},{6,7},{7,6},{8,9},{9,8},{10,11... | collective-permute-start | bytes 786440 | tf_op jit(solution)/shard_map/ppermute | solution.py:186
  4.1 7.9 %collective-permute-start.1 = (bf16[128,1024]{1,0:T(8,128)(2,1)S(1)}, bf16[128,1024]{1,0:T(8,128)(2,1)S(1)}, u32[]{:S(2)}, u32[]{:S(2)}) collective-permute-start(bf16[128,1024]{1,0:T(8,128)(2,1)S(1)} %constant_dynamic-update-slice_fusion.refs_0_.refs_1_), channel_id=1, source_target_pairs={{0,8},{4,12},{8,16},{12,20},{16,24},{20,28},{24,0},{28,4},{1,9},{5... | collective-permute-start | bytes 786440 | tf_op jit(solution)/shard_map/ppermute | solution.py:193
  4.1 7.9 %collective-permute-start = (bf16[128,1024]{1,0:T(8,128)(2,1)S(1)}, bf16[128,1024]{1,0:T(8,128)(2,1)S(1)}, u32[]{:S(2)}, u32[]{:S(2)}) collective-permute-start(bf16[128,1024]{1,0:T(8,128)(2,1)S(1)} %constant_dynamic-update-slice_fusion.refs_0_.refs_1_), channel_id=1, source_target_pairs={{0,4},{4,0},{8,12},{12,8},{16,20},{20,16},{24,28},{28,24},{1,5},{5... | collective-permute-start | bytes 786440 | tf_op jit(solution)/shard_map/ppermute | solution.py:195
  12.0 0.7 copy-start.26
  12.1 0.8 copy-start.27
  22.6 7.3 %collective-permute-start.8 = (bf16[128,1024]{1,0:T(8,128)(2,1)}, bf16[128,1024]{1,0:T(8,128)(2,1)S(1)}, u32[]{:S(2)}, u32[]{:S(2)}) collective-permute-start(bf16[128,1024]{1,0:T(8,128)(2,1)} %shard_map.74.refs_8_.refs_9_), channel_id=1, source_target_pairs={{0,2},{1,3},{2,0},{3,1},{4,6},{5,7},{6,4},{7,5},{8,10},{9,11},{10,... | collective-permute-start | bytes 786440 | tf_op jit(solution)/shard_map/ppermute | solution.py:204
  22.9 7.0 %collective-permute-start.7 = (bf16[128,1024]{1,0:T(8,128)(2,1)}, bf16[128,1024]{1,0:T(8,128)(2,1)S(1)}, u32[]{:S(2)}, u32[]{:S(2)}) collective-permute-start(bf16[128,1024]{1,0:T(8,128)(2,1)} %shard_map.74.refs_8_.refs_9_), channel_id=1, source_target_pairs={{0,1},{1,0},{2,3},{3,2},{4,5},{5,4},{6,7},{7,6},{8,9},{9,8},{10,11... | collective-permute-start | bytes 786440 | tf_op jit(solution)/shard_map/ppermute | solution.py:186
  23.9 6.0 %collective-permute-start.6 = (bf16[128,1024]{1,0:T(8,128)(2,1)S(1)}, bf16[128,1024]{1,0:T(8,128)(2,1)S(1)}, u32[]{:S(2)}, u32[]{:S(2)}) collective-permute-start(bf16[128,1024]{1,0:T(8,128)(2,1)S(1)} %collective-permute-done.3.refs_4_.refs_5_), channel_id=1, source_target_pairs={{0,1},{1,0},{2,3},{3,2},{4,5},{5,4},{6,7},{7,6},{8,9},{9,8},{10,11... | collective-permute-start | bytes 786440 | tf_op jit(solution)/shard_map/ppermute | solution.py:186
  23.9 7.6 %collective-permute-start.5 = (bf16[128,1024]{1,0:T(8,128)(2,1)}, bf16[128,1024]{1,0:T(8,128)(2,1)S(1)}, u32[]{:S(2)}, u32[]{:S(2)}) collective-permute-start(bf16[128,1024]{1,0:T(8,128)(2,1)} %copy-done.26), channel_id=1, source_target_pairs={{0,8},{4,12},{8,16},{12,20},{16,24},{20,28},{24,0},{28,4},{1,9},{5... | collective-permute-start | bytes 786440 | tf_op jit(solution)/shard_map/ppermute | solution.py:193
  25.7 7.3 %collective-permute-start.4 = (bf16[128,1024]{1,0:T(8,128)(2,1)}, bf16[128,1024]{1,0:T(8,128)(2,1)S(1)}, u32[]{:S(2)}, u32[]{:S(2)}) collective-permute-start(bf16[128,1024]{1,0:T(8,128)(2,1)} %copy-done.26), channel_id=1, source_target_pairs={{0,4},{4,0},{8,12},{12,8},{16,20},{20,16},{24,28},{28,24},{1,5},{5... | collective-permute-start | bytes 786440 | tf_op jit(solution)/shard_map/ppermute | solution.py:195
  29.9 37.0 %copy-start.12 = (bf16[128,1024]{1,0:T(8,128)(2,1)}, bf16[128,1024]{1,0:T(8,128)(2,1)S(1)}, u32[]{:S(2)}) copy-start(bf16[128,1024]{1,0:T(8,128)(2,1)S(1)} %collective-permute-done.8.refs_12_.refs_13_) | copy-start | bytes 786436
  29.9 37.0 %copy-start.14 = (bf16[128,1024]{1,0:T(8,128)(2,1)}, bf16[128,1024]{1,0:T(8,128)(2,1)S(1)}, u32[]{:S(2)}) copy-start(bf16[128,1024]{1,0:T(8,128)(2,1)S(1)} %collective-permute-done.7.refs_10_.refs_11_) | copy-start | bytes 786436
  29.9 37.0 %copy-start.16 = (bf16[128,1024]{1,0:T(8,128)(2,1)}, bf16[128,1024]{1,0:T(8,128)(2,1)S(1)}, u32[]{:S(2)}) copy-start(bf16[128,1024]{1,0:T(8,128)(2,1)S(1)} %collective-permute-done.6.refs_6_.refs_7_) | copy-start | bytes 786436
  31.5 1.5 copy-start.28
  33.0 0.7 copy-start.29
  43.4 7.0 %collective-permute-start.13 = (bf16[128,1024]{1,0:T(8,128)(2,1)}, bf16[128,1024]{1,0:T(8,128)(2,1)S(1)}, u32[]{:S(2)}, u32[]{:S(2)}) collective-permute-start(bf16[128,1024]{1,0:T(8,128)(2,1)} %shard_map.75.refs_16_.refs_17_), channel_id=1, source_target_pairs={{0,2},{1,3},{2,0},{3,1},{4,6},{5,7},{6,4},{7,5},{8,10},{9,11},{10,... | collective-permute-start | bytes 786440 | tf_op jit(solution)/shard_map/ppermute | solution.py:204
  44.7 5.7 %collective-permute-start.12 = (bf16[128,1024]{1,0:T(8,128)(2,1)}, bf16[128,1024]{1,0:T(8,128)(2,1)S(1)}, u32[]{:S(2)}, u32[]{:S(2)}) collective-permute-start(bf16[128,1024]{1,0:T(8,128)(2,1)} %shard_map.75.refs_16_.refs_17_), channel_id=1, source_target_pairs={{0,1},{1,0},{2,3},{3,2},{4,5},{5,4},{6,7},{7,6},{8,9},{9,8},{10,11... | collective-permute-start | bytes 786440 | tf_op jit(solution)/shard_map/ppermute | solution.py:186
  46.7 4.5 %collective-permute-start.11 = (bf16[128,1024]{1,0:T(8,128)(2,1)S(1)}, bf16[128,1024]{1,0:T(8,128)(2,1)S(1)}, u32[]{:S(2)}, u32[]{:S(2)}) collective-permute-start(bf16[128,1024]{1,0:T(8,128)(2,1)S(1)} %collective-permute-done.8.refs_12_.refs_13_), channel_id=1, source_target_pairs={{0,1},{1,0},{2,3},{3,2},{4,5},{5,4},{6,7},{7,6},{8,9},{9,8},{10,11... | collective-permute-start | bytes 786440 | tf_op jit(solution)/shard_map/ppermute | solution.py:186
  46.7 8.0 %collective-permute-start.10 = (bf16[128,1024]{1,0:T(8,128)(2,1)}, bf16[128,1024]{1,0:T(8,128)(2,1)S(1)}, u32[]{:S(2)}, u32[]{:S(2)}) collective-permute-start(bf16[128,1024]{1,0:T(8,128)(2,1)} %copy-done.28), channel_id=1, source_target_pairs={{0,8},{4,12},{8,16},{12,20},{16,24},{20,28},{24,0},{28,4},{1,9},{5... | collective-permute-start | bytes 786440 | tf_op jit(solution)/shard_map/ppermute | solution.py:193
  49.2 7.3 %collective-permute-start.9 = (bf16[128,1024]{1,0:T(8,128)(2,1)}, bf16[128,1024]{1,0:T(8,128)(2,1)S(1)}, u32[]{:S(2)}, u32[]{:S(2)}) collective-permute-start(bf16[128,1024]{1,0:T(8,128)(2,1)} %copy-done.28), channel_id=1, source_target_pairs={{0,4},{4,0},{8,12},{12,8},{16,20},{20,16},{24,28},{28,24},{1,5},{5... | collective-permute-start | bytes 786440 | tf_op jit(solution)/shard_map/ppermute | solution.py:195
  50.4 6.0 %copy-start.18 = (bf16[128,1024]{1,0:T(8,128)(2,1)}, bf16[128,1024]{1,0:T(8,128)(2,1)S(1)}, u32[]{:S(2)}) copy-start(bf16[128,1024]{1,0:T(8,128)(2,1)S(1)} %collective-permute-done.13.refs_20_.refs_21_) | copy-start | bytes 786436
  50.4 0.7 copy-start.20
  51.2 16.1 %copy-start.22 = (bf16[128,1024]{1,0:T(8,128)(2,1)}, bf16[128,1024]{1,0:T(8,128)(2,1)S(1)}, u32[]{:S(2)}) copy-start(bf16[128,1024]{1,0:T(8,128)(2,1)S(1)} %collective-permute-done.11.refs_14_.refs_15_) | copy-start | bytes 786436
  54.7 1.8 %copy-start.30 = (bf16[128,1024]{1,0:T(8,128)(2,1)}, bf16[128,1024]{1,0:T(8,128)(2,1)S(1)}, u32[]{:S(2)}) copy-start(bf16[128,1024]{1,0:T(8,128)(2,1)S(1)} %collective-permute-done.10.refs_6_) | copy-start | bytes 786436
  56.5 0.7 copy-start.31
  66.9 10.0 %copy-start.3 = (bf16[128,1024]{1,0:T(8,128)(2,1)S(1)}, bf16[128,1024]{1,0:T(8,128)(2,1)}, u32[]{:S(2)}) copy-start(bf16[128,1024]{1,0:T(8,128)(2,1)} %shard_map.76.refs_2_.refs_3_) | copy-start | bytes 786436
  66.9 13.9 %collective-permute-start.17 = (bf16[128,1024]{1,0:T(8,128)(2,1)}, bf16[128,1024]{1,0:T(8,128)(2,1)S(1)}, u32[]{:S(2)}, u32[]{:S(2)}) collective-permute-start(bf16[128,1024]{1,0:T(8,128)(2,1)} %shard_map.76.refs_2_.refs_3_), channel_id=1, source_target_pairs={{0,2},{1,3},{2,0},{3,1},{4,6},{5,7},{6,4},{7,5},{8,10},{9,11},{10,... | collective-permute-start | bytes 786440 | tf_op jit(solution)/shard_map/ppermute | solution.py:204
  77.0 30.5 %copy-start.1 = (bf16[128,1024]{1,0:T(8,128)(2,1)S(1)}, bf16[128,1024]{1,0:T(8,128)(2,1)}, u32[]{:S(2)}) copy-start(bf16[128,1024]{1,0:T(8,128)(2,1)} %copy-done) | copy-start | bytes 786436
  77.0 30.5 %copy-start.2 = (bf16[128,3072]{1,0:T(8,128)(2,1)S(1)}, bf16[128,3072]{1,0:T(8,128)(2,1)}, u32[]{:S(2)}) copy-start(bf16[128,3072]{1,0:T(8,128)(2,1)} %q_ref.5) | copy-start | bytes 2359300
  77.0 30.5 %copy-start.6 = (bf16[128,1024]{1,0:T(8,128)(2,1)S(1)}, bf16[128,1024]{1,0:T(8,128)(2,1)}, u32[]{:S(2)}) copy-start(bf16[128,1024]{1,0:T(8,128)(2,1)} %shard_map.74.refs_8_.refs_9_) | copy-start | bytes 786436
  77.0 30.5 %copy-start.7 = (bf16[128,1024]{1,0:T(8,128)(2,1)S(1)}, bf16[128,1024]{1,0:T(8,128)(2,1)}, u32[]{:S(2)}) copy-start(bf16[128,1024]{1,0:T(8,128)(2,1)} %shard_map.75.refs_16_.refs_17_) | copy-start | bytes 786436
  77.0 30.5 %copy-start.8 = (f32[8,24]{1,0:T(8,128)S(1)}, f32[8,24]{1,0:T(8,128)}, u32[]{:S(2)}) copy-start(f32[8,24]{1,0:T(8,128)} %temps_ref.5) | copy-start | bytes 2308
  77.0 30.4 %copy-start.9 = (s32[2]{0:T(128)S(1)}, s32[2]{0:T(128)}, u32[]{:S(2)}) copy-start(s32[2]{0:T(128)} %pad_add_fusion.where_ref) | copy-start | bytes 28
  77.0 30.4 %copy-start.10 = (s32[8]{0:T(128)S(1)}, s32[8]{0:T(128)}, u32[]{:S(2)}) copy-start(s32[8]{0:T(128)} %levels_ref.5) | copy-start | bytes 100
  77.1 30.4 %copy-start.11 = (s32[6]{0:T(128)S(1)}, s32[6]{0:T(128)}, u32[]{:S(2)}) copy-start(s32[6]{0:T(128)} %get-tuple-element.73.count_ref) | copy-start | bytes 76
  77.1 5.0 %collective-permute-start.16 = (bf16[128,1024]{1,0:T(8,128)(2,1)S(1)}, bf16[128,1024]{1,0:T(8,128)(2,1)S(1)}, u32[]{:S(2)}, u32[]{:S(2)}) collective-permute-start(bf16[128,1024]{1,0:T(8,128)(2,1)S(1)} %copy-done.3), channel_id=1, source_target_pairs={{0,1},{1,0},{2,3},{3,2},{4,5},{5,4},{6,7},{7,6},{8,9},{9,8},{10,11... | collective-permute-start | bytes 786440 | tf_op jit(solution)/shard_map/ppermute | solution.py:186
  79.1 8.2 %collective-permute-start.19 = (bf16[128,1024]{1,0:T(8,128)(2,1)}, bf16[128,1024]{1,0:T(8,128)(2,1)S(1)}, u32[]{:S(2)}, u32[]{:S(2)}) collective-permute-start(bf16[128,1024]{1,0:T(8,128)(2,1)} %shard_map.77.refs_10_.refs_11_), channel_id=1, source_target_pairs={{0,2},{1,3},{2,0},{3,1},{4,6},{5,7},{6,4},{7,5},{8,10},{9,11},{10,... | collective-permute-start | bytes 786440 | tf_op jit(solution)/shard_map/ppermute | solution.py:204
  80.3 7.0 %collective-permute-start.18 = (bf16[128,1024]{1,0:T(8,128)(2,1)}, bf16[128,1024]{1,0:T(8,128)(2,1)S(1)}, u32[]{:S(2)}, u32[]{:S(2)}) collective-permute-start(bf16[128,1024]{1,0:T(8,128)(2,1)} %shard_map.77.refs_10_.refs_11_), channel_id=1, source_target_pairs={{0,1},{1,0},{2,3},{3,2},{4,5},{5,4},{6,7},{7,6},{8,9},{9,8},{10,11... | collective-permute-start | bytes 786440 | tf_op jit(solution)/shard_map/ppermute | solution.py:186
  80.7 6.6 %collective-permute-start.15 = (bf16[128,1024]{1,0:T(8,128)(2,1)}, bf16[128,1024]{1,0:T(8,128)(2,1)S(1)}, u32[]{:S(2)}, u32[]{:S(2)}) collective-permute-start(bf16[128,1024]{1,0:T(8,128)(2,1)} %copy-done.18), channel_id=1, source_target_pairs={{0,1},{1,0},{2,3},{3,2},{4,5},{5,4},{6,7},{7,6},{8,9},{9,8},{10,11... | collective-permute-start | bytes 786440 | tf_op jit(solution)/shard_map/ppermute | solution.py:186
  80.9 7.9 %collective-permute-start.14 = (bf16[128,1024]{1,0:T(8,128)(2,1)}, bf16[128,1024]{1,0:T(8,128)(2,1)}, u32[]{:S(2)}, u32[]{:S(2)}) collective-permute-start(bf16[128,1024]{1,0:T(8,128)(2,1)} %copy-done.30), channel_id=1, source_target_pairs={{0,4},{4,0},{8,12},{12,8},{16,20},{20,16},{24,28},{28,24},{1,5},{5... | collective-permute-start | bytes 786440 | tf_op jit(solution)/shard_map/ppermute | solution.py:195
  87.3 0.7 copy-start.24
  98.5 6.9 %collective-permute-start.23 = (bf16[128,1024]{1,0:T(8,128)(2,1)}, bf16[128,1024]{1,0:T(8,128)(2,1)S(1)}, u32[]{:S(2)}, u32[]{:S(2)}) collective-permute-start(bf16[128,1024]{1,0:T(8,128)(2,1)} %shard_map.80.refs_2_.refs_3_), channel_id=1, source_target_pairs={{0,2},{1,3},{2,0},{3,1},{4,6},{5,7},{6,4},{7,5},{8,10},{9,11},{10,... | collective-permute-start | bytes 786440 | tf_op jit(solution)/shard_map/ppermute | solution.py:204
  99.0 28.3 %collective-permute-start.20 = (bf16[128,1024]{1,0:T(8,128)(2,1)S(1)}, bf16[128,1024]{1,0:T(8,128)(2,1)S(1)}, u32[]{:S(2)}, u32[]{:S(2)}) collective-permute-start(bf16[128,1024]{1,0:T(8,128)(2,1)S(1)} %collective-permute-done.17.refs_6_.refs_7_), channel_id=1, source_target_pairs={{0,1},{1,0},{2,3},{3,2},{4,5},{5,4},{6,7},{7,6},{8,9},{9,8},{10,11... | collective-permute-start | bytes 786440 | tf_op jit(solution)/shard_map/ppermute | solution.py:186
  100.2 27.2 %collective-permute-start.21 = (bf16[128,1024]{1,0:T(8,128)(2,1)S(1)}, bf16[128,1024]{1,0:T(8,128)(2,1)S(1)}, u32[]{:S(2)}, u32[]{:S(2)}) collective-permute-start(bf16[128,1024]{1,0:T(8,128)(2,1)S(1)} %collective-permute-done.19.refs_14_.refs_15_), channel_id=1, source_target_pairs={{0,1},{1,0},{2,3},{3,2},{4,5},{5,4},{6,7},{7,6},{8,9},{9,8},{10,11... | collective-permute-start | bytes 786440 | tf_op jit(solution)/shard_map/ppermute | solution.py:186
  100.2 41.2 %collective-permute-start.22 = (bf16[128,1024]{1,0:T(8,128)(2,1)}, bf16[128,1024]{1,0:T(8,128)(2,1)S(1)}, u32[]{:S(2)}, u32[]{:S(2)}) collective-permute-start(bf16[128,1024]{1,0:T(8,128)(2,1)} %shard_map.80.refs_2_.refs_3_), channel_id=1, source_target_pairs={{0,1},{1,0},{2,3},{3,2},{4,5},{5,4},{6,7},{7,6},{8,9},{9,8},{10,11... | collective-permute-start | bytes 786440 | tf_op jit(solution)/shard_map/ppermute | solution.py:186
  105.4 36.1 %collective-permute-start.24 = (bf16[128,1024]{1,0:T(8,128)(2,1)S(1)}, bf16[128,1024]{1,0:T(8,128)(2,1)S(1)}, u32[]{:S(2)}, u32[]{:S(2)}) collective-permute-start(bf16[128,1024]{1,0:T(8,128)(2,1)S(1)} %collective-permute-done.23.refs_6_.refs_7_), channel_id=1, source_target_pairs={{0,1},{1,0},{2,3},{3,2},{4,5},{5,4},{6,7},{7,6},{8,9},{9,8},{10,11... | collective-permute-start | bytes 786440 | tf_op jit(solution)/shard_map/ppermute | solution.py:186
  107.5 1.0 copy-start.13
  108.5 0.9 copy-start.15
  109.4 0.9 copy-start.17
  110.4 0.9 copy-start.19
  111.3 0.9 copy-start.21
  112.3 0.9 copy-start.23
  113.2 0.9 copy-start.25
  114.2 13.2 %copy-start.4 = (bf16[128,1024]{1,0:T(8,128)(2,1)S(1)}, bf16[128,1024]{1,0:T(8,128)(2,1)}, u32[]{:S(2)}) copy-start(bf16[128,1024]{1,0:T(8,128)(2,1)} %shard_map.77.refs_10_.refs_11_) | copy-start | bytes 786436
  127.4 14.0 %copy-start.5 = (bf16[128,1024]{1,0:T(8,128)(2,1)S(1)}, bf16[128,1024]{1,0:T(8,128)(2,1)}, u32[]{:S(2)}) copy-start(bf16[128,1024]{1,0:T(8,128)(2,1)} %shard_map.80.refs_2_.refs_3_) | copy-start | bytes 786436
